TPU v7x, 128 devices: a whole 4x4x4 slice. The times are simulated.
128 devices in a mesh: tm: 16 (over x_lo, y, core), patch: 8 (over z, x_hi).
Axes of the slice: x: 4 (x_hi: 2, x_lo: 2; x = x_hi * 2 + x_lo), y: 4, z: 4, core: 2. Of those that a mesh axis runs over, the one named last changes fastest.
Arguments:
- frames_in: bfloat16 [128, 512, 1024], P('tm', 'patch'), may hold values from -6 to 6
- codes: int32 [128, 512], P('tm', 'patch'), may hold values from 0 to 1023
- gain_space: float32 [1024], replicated, may hold values from 0.1 to 1.9
- qkv_space: bfloat16 [1024, 3072], replicated, may hold values from -0.1875 to 0.1875
- out_space: bfloat16 [1024, 1024], replicated, may hold values from -0.75 to 0.75
- scale_space: float32 [16], replicated, may hold values from 3 to 12
- gain_time: float32 [1024], replicated, may hold values from 0.1 to 1.9
- qkv_time: bfloat16 [1024, 3072], replicated, may hold values from -0.1875 to 0.1875
- out_time: bfloat16 [1024, 1024], replicated, may hold values from -0.75 to 0.75
- scale_time: float32 [16], replicated, may hold values from 3 to 12
- codebook: bfloat16 [1024, 1024], replicated, may hold values from -6 to 6
Outputs:
- encoded: bfloat16 [128, 512, 1024], P('tm', 'patch')
- commitment: bfloat16 [128, 512, 1024], P('tm', 'patch')
All inputs are finite; a program needn't handle non-finite values.
Results may differ from a plain program's by a relative error of at most 0.02.
Values may be sent and summed in bfloat16 or wider, within the bound.
No kernel may reach another device: no remote copies, remote signals or barrier semaphores. Data moves between devices by JAX's collectives and lax.ppermute only.
A program may use at most 192 MiB of HBM per device.

v0:
```python
import functools
import math

import jax
import jax.numpy as jnp
from jax import lax
from jax.experimental import pallas as pl
from jax.experimental.pallas import tpu as pltpu
from jax.sharding import PartitionSpec as P

H = 16
HD = 64
D = 1024
GROUP = 256
PAIR = 128
LOG2E = math.log2(math.e)
VMEM_LIMIT = 48 * 1024 * 1024
f32 = jnp.float32
bf16 = jnp.bfloat16


def iota(shape, axis):
    return lax.broadcasted_iota(jnp.int32, shape, axis)


def same_head_mean():
    same = (iota((GROUP, GROUP), 0) // HD) == (iota((GROUP, GROUP), 1) // HD)
    return jnp.where(same, f32(1.0 / HD), f32(0.0)).astype(bf16)


def norm_rows(wide, gain):
    mean = jnp.mean(wide * wide, -1, keepdims=True)
    return (wide * lax.rsqrt(mean + 1e-5) * gain).astype(bf16)


def head_norm(block, averager):
    square = (block * block).astype(bf16)
    mean = jnp.dot(square, averager, preferred_element_type=f32)
    return block * lax.rsqrt(mean + 1e-6)


def scale_row(scale_ref, first_head):
    head = iota((1, GROUP), 1) // HD
    row = jnp.full((1, GROUP), scale_ref[first_head], f32)
    for h in range(1, GROUP // HD):
        row = jnp.where(head == h, scale_ref[first_head + h], row)
    return row * f32(LOG2E / HD)


def key_pair(key):
    low = iota(key.shape, 1) < HD
    zero = jnp.zeros_like(key)
    return jnp.concatenate([jnp.where(low, key, zero), jnp.where(low, zero, key)], 0)


def value_pair(value):
    low = iota(value.shape, 1) < HD
    zero = jnp.zeros_like(value)
    one = jnp.ones_like(value)
    first = jnp.concatenate([jnp.where(low, value, zero), jnp.where(low, one, zero)], 1)
    second = jnp.concatenate([jnp.where(low, zero, value), jnp.where(low, zero, one)], 1)
    return jnp.concatenate([first, second], 0)


def weight_copies(qkv_hbm, qkv_buf, sems):
    copies = []
    for part in range(3):
        for g in range(D // GROUP):
            copies.append(
                pltpu.make_async_copy(
                    qkv_hbm.at[:, pl.ds(part * D + g * GROUP, GROUP)],
                    qkv_buf.at[:, pl.ds(part * D + g * GROUP, GROUP)],
                    sems.at[part, g],
                )
            )
    return copies


def spatial_kernel(x_ref, gain_ref, scale_ref, qkv_hbm, out_hbm, o_ref, qkv_buf, out_buf, normed, attn, sems, out_sem):
    copies = weight_copies(qkv_hbm, qkv_buf, sems)
    for g in range(4):
        for part in range(3):
            copies[part * 4 + g].start()
    out_copy = pltpu.make_async_copy(out_hbm, out_buf, out_sem)
    out_copy.start()
    normed[...] = norm_rows(x_ref[...].astype(f32), gain_ref[...])
    averager = same_head_mean()
    for g in range(4):
        for part in range(3):
            copies[part * 4 + g].wait()
        src = normed[...]
        col = g * GROUP
        q = jnp.dot(src, qkv_buf[:, col : col + GROUP], preferred_element_type=f32)
        k = jnp.dot(src, qkv_buf[:, D + col : D + col + GROUP], preferred_element_type=f32)
        v = jnp.dot(src, qkv_buf[:, 2 * D + col : 2 * D + col + GROUP], preferred_element_type=f32)
        q = (head_norm(q, averager) * scale_row(scale_ref, 4 * g)).astype(bf16)
        k = head_norm(k, averager).astype(bf16)
        v = v.astype(bf16)
        for pair in range(2):
            lanes = slice(pair * PAIR, (pair + 1) * PAIR)
            keys = key_pair(k[:, lanes])
            values = value_pair(v[:, lanes])
            for r in range(2):
                rows = slice(r * 256, (r + 1) * 256)
                s = lax.dot_general(q[rows, lanes], keys, (((1,), (1,)), ((), ())), preferred_element_type=f32)
                w = jnp.exp2(s).astype(bf16)
                o = jnp.dot(w, values, preferred_element_type=f32)
                attn[rows, col + pair * PAIR : col + (pair + 1) * PAIR] = (o[:, :PAIR] / o[:, PAIR:]).astype(bf16)
    out_copy.wait()
    half = D // 2
    low = iota((1, 8, half), 1) < 4
    stream = x_ref[...].astype(f32) + jnp.dot(attn[...], out_buf[...], preferred_element_type=f32)
    a = stream[:, :half].reshape(64, 8, half)
    b = stream[:, half:].reshape(64, 8, half)
    even = jnp.where(low, a, pltpu.roll(b, 4, 1)).astype(bf16)
    odd = jnp.where(low, pltpu.roll(a, 4, 1), b).astype(bf16)
    for j in range(8):
        o_ref[:, j] = jnp.stack([even[8 * j : 8 * j + 8], odd[8 * j : 8 * j + 8]], 1).reshape(16, 8, half)


def temporal_kernel(x_ref, gain_ref, scale_ref, qkv_hbm, out_hbm, o_ref, qkv_buf, out_buf, stream, normed, attn, sems, out_sem):
    copies = weight_copies(qkv_hbm, qkv_buf, sems)
    for g in range(4):
        for part in range(3):
            copies[part * 4 + g].start()
    out_copy = pltpu.make_async_copy(out_hbm, out_buf, out_sem)
    out_copy.start()
    half = D // 2
    want = iota((512, 1024), 0)
    have = iota((512, 1024), 1)
    source = (want & 127) * 8 + (want >> 7)
    recv = x_ref[...].reshape(1024, half)
    one = f32(1.0)
    nil = f32(0.0)
    stream[:, :half] = jnp.dot(jnp.where(have == source, one, nil).astype(bf16), recv, preferred_element_type=f32)
    stream[:, half:] = jnp.dot(jnp.where(have == source + 4, one, nil).astype(bf16), recv, preferred_element_type=f32)
    normed[...] = norm_rows(stream[...], gain_ref[...])
    averager = same_head_mean()
    causal = iota((128, 256), 0) >= (iota((128, 256), 1) & 127)
    for g in range(4):
        for part in range(3):
            copies[part * 4 + g].wait()
        src = normed[...]
        col = g * GROUP
        q = jnp.dot(src, qkv_buf[:, col : col + GROUP], preferred_element_type=f32)
        k = jnp.dot(src, qkv_buf[:, D + col : D + col + GROUP], preferred_element_type=f32)
        v = jnp.dot(src, qkv_buf[:, 2 * D + col : 2 * D + col + GROUP], preferred_element_type=f32)
        q = (head_norm(q, averager) * scale_row(scale_ref, 4 * g)).astype(bf16)
        k = head_norm(k, averager).astype(bf16)
        v = v.astype(bf16)
        for pair in range(2):
            lanes = slice(pair * PAIR, (pair + 1) * PAIR)
            for p in range(4):
                rows = slice(p * 128, (p + 1) * 128)
                keys = key_pair(k[rows, lanes])
                values = value_pair(v[rows, lanes])
                s = lax.dot_general(q[rows, lanes], keys, (((1,), (1,)), ((), ())), preferred_element_type=f32)
                w = jnp.where(causal, jnp.exp2(s), nil).astype(bf16)
                o = jnp.dot(w, values, preferred_element_type=f32)
                attn[rows, col + pair * PAIR : col + (pair + 1) * PAIR] = (o[:, :PAIR] / o[:, PAIR:]).astype(bf16)
    out_copy.wait()
    output = (stream[...] + jnp.dot(attn[...], out_buf[...], preferred_element_type=f32)).astype(bf16)
    want = iota((512, 512), 0)
    source = (want & 3) * 128 + (want >> 2)
    move = jnp.where(iota((512, 512), 1) == source, one, nil).astype(bf16)
    o_ref[...] = jnp.dot(move, output, preferred_element_type=f32).astype(bf16)


def chosen_kernel(codes_ref, codebook_ref, o_ref):
    hot = jnp.where(codes_ref[...] == iota((512, D), 1), f32(1.0), f32(0.0)).astype(bf16)
    o_ref[...] = jnp.dot(hot, codebook_ref[...], preferred_element_type=f32).astype(bf16)


def final_kernel(x_ref, chosen_ref, enc_ref, com_ref):
    want = iota((512, 512), 0)
    source = ((want >> 2) & 15) * 32 + (want >> 6) * 4 + (want & 3)
    move = jnp.where(iota((512, 512), 1) == source, f32(1.0), f32(0.0)).astype(bf16)
    output = jnp.dot(move, x_ref[...], preferred_element_type=f32)
    enc_ref[...] = output.astype(bf16)
    com_ref[...] = (output - chosen_ref[...].astype(f32)).astype(bf16)


VM = pl.BlockSpec(memory_space=pltpu.VMEM)
SM = pl.BlockSpec(memory_space=pltpu.SMEM)
ANY = pl.BlockSpec(memory_space=pl.ANY)
PARAMS = pltpu.CompilerParams(vmem_limit_bytes=VMEM_LIMIT)


def cost(gmac, mbytes):
    return pl.CostEstimate(flops=int(2e9 * gmac), bytes_accessed=int(1e6 * mbytes), transcendentals=0)


def weight_scratch():
    return [pltpu.VMEM((D, 3 * D), bf16), pltpu.VMEM((D, D), bf16)]


def shards(frames_in, codes, gain_space, qkv_space, out_space, scale_space, gain_time, qkv_time, out_time, scale_time, codebook):
    x = lax.all_to_all(frames_in, "patch", 0, 0, tiled=True).reshape(512, D)
    chosen = pl.pallas_call(
        chosen_kernel,
        out_shape=jax.ShapeDtypeStruct((512, D), bf16),
        in_specs=[VM, VM],
        out_specs=VM,
        compiler_params=PARAMS,
        cost_estimate=cost(0.6, 6),
        name="chosen",
    )(codes.reshape(512, 1), codebook)
    sems = [pltpu.SemaphoreType.DMA((3, 4)), pltpu.SemaphoreType.DMA]
    stream = pl.pallas_call(
        spatial_kernel,
        out_shape=jax.ShapeDtypeStruct((16, 8, 8, 512), bf16),
        in_specs=[VM, VM, SM, ANY, ANY],
        out_specs=VM,
        scratch_shapes=weight_scratch() + [pltpu.VMEM((512, D), bf16)] * 2 + sems,
        compiler_params=PARAMS,
        cost_estimate=cost(5, 10),
        name="spatial",
    )(x, gain_space.reshape(1, D), scale_space, qkv_space, out_space)
    stream = lax.all_to_all(stream.reshape(128, 8, 512), ("tm", "patch"), 0, 0, tiled=True)
    output = pl.pallas_call(
        temporal_kernel,
        out_shape=jax.ShapeDtypeStruct((512, D), bf16),
        in_specs=[VM, VM, SM, ANY, ANY],
        out_specs=VM,
        scratch_shapes=weight_scratch() + [pltpu.VMEM((512, D), f32)] + [pltpu.VMEM((512, D), bf16)] * 2 + sems,
        compiler_params=PARAMS,
        cost_estimate=cost(4, 10),
        name="temporal",
    )(stream, gain_time.reshape(1, D), scale_time, qkv_time, out_time)
    output = lax.all_to_all(output.reshape(16, 32, D), "tm", 0, 0, tiled=True).reshape(512, D)
    encoded, commitment = pl.pallas_call(
        final_kernel,
        out_shape=[jax.ShapeDtypeStruct((512, D), bf16)] * 2,
        in_specs=[VM, VM],
        out_specs=[VM, VM],
        compiler_params=PARAMS,
        cost_estimate=cost(0.3, 4),
        name="final",
    )(output, chosen)
    return encoded.reshape(8, 64, D), commitment.reshape(8, 64, D)


def solution(mesh):
    rows = P("tm", "patch", None)
    return jax.shard_map(
        shards,
        mesh=mesh,
        in_specs=(rows, P("tm", "patch")) + (P(),) * 9,
        out_specs=(rows, rows),
        check_vma=False,
    )
```

profile of v0, /device:TPU:1, one launch (start us, length us, event | category | flops | bytes accessed | tf_op | source)
XLA Modules:
  0.0 101.1 jit_solution(12836042811498415860)
XLA Ops:
  0.6 0.0 copy-start.5
  0.6 0.0 copy-start
  0.6 24.8 %all_to_all.15 = bf16[8,64,1024]{2,1,0:T(8,128)(2,1)S(1)} all-to-all(bf16[8,64,1024]{2,1,0:T(8,128)(2,1)} %param.11), channel_id=1, replica_groups=mesh['tm'=16,'patch'=8] {'patch'}, dimensions={0} | all-to-all | bytes 2097152 | tf_op jit(solution)/shard_map/all_to_all | solution.py:198
  25.4 0.0 copy-done.5
  25.4 0.0 copy-done
  25.4 0.0 copy-start.3
  25.4 0.7 copy-done.3
  26.1 0.0 copy-start.4
  26.1 13.1 %spatial.1 = bf16[16,8,8,512]{3,2,1,0:T(8,128)(2,1)S(1)} custom-call(bf16[512,1024]{1,0:T(8,128)(2,1)S(1)} %bitcast.10, f32[1,1024]{1,0:T(1,128)S(1)} %bitcast.11, f32[16]{0:T(128)S(1)} %copy-done.5, bf16[1024,3072]{1,0:T(8,128)(2,1)} %qkv_hbm.2, bf16[1024,1024]{1,0:T(8,128)(2,1)S(1)} %copy-done), custom_call_target="tpu_custom_call" | custom-call | flops 10000000000 | bytes 10000000 | tf_op jit(solution)/shard_map/spatial/pallas_call | solution.py:209
  39.2 0.0 copy-start.1
  39.2 0.0 copy-start.6
  39.2 24.5 %all_to_all.16.x_ref = bf16[128,8,512]{2,1,0:T(8,128)(2,1)S(1)} all-to-all(bf16[128,8,512]{2,1,0:T(8,128)(2,1)S(1)} %bitcast.9), channel_id=1, replica_groups=mesh['tm'=16,'patch'=8] {'tm','patch'}, dimensions={0} | all-to-all | bytes 2097152 | tf_op jit(solution)/shard_map/all_to_all | solution.py:219
  63.8 0.0 copy-done.4
  63.8 0.0 copy-done.1
  63.8 0.0 copy-done.6
  63.8 0.0 copy-start.9
  63.8 12.9 %temporal.1 = bf16[512,1024]{1,0:T(8,128)(2,1)} custom-call(bf16[128,8,512]{2,1,0:T(8,128)(2,1)S(1)} %all_to_all.16.x_ref, f32[1,1024]{1,0:T(1,128)S(1)} %bitcast.12, f32[16]{0:T(128)S(1)} %copy-done.6, bf16[1024,3072]{1,0:T(8,128)(2,1)} %qkv_hbm.3, bf16[1024,1024]{1,0:T(8,128)(2,1)S(1)} %copy-done.1), custom_call_target="tpu_custom_call" | custom-call | flops 8000000000 | bytes 10000000 | tf_op jit(solution)/shard_map/temporal/pallas_call | solution.py:220
  76.7 0.0 copy-start.2
  76.7 5.2 %all-to-all-start.2 = ((bf16[16,32,1024]{2,1,0:T(8,128)(2,1)}), bf16[16,32,1024]{2,1,0:T(8,128)(2,1)S(1)}, u32[]{:S(2)}, u32[]{:S(2)}) async-start(bf16[16,32,1024]{2,1,0:T(8,128)(2,1)} %bitcast.4), calls=%async_computation.2 | async-start | bytes 2097152 | tf_op jit(solution)/shard_map/all_to_all | solution.py:230
  81.9 0.0 copy-done.9
  81.9 0.2 reshape.40.codes_ref
  82.1 0.0 copy-done.2
  82.2 1.3 %chosen.1.chosen_ref = bf16[512,1024]{1,0:T(8,128)(2,1)S(1)} custom-call(s32[512,1]{1,0:T(8,128)S(1)} %reshape.40.codes_ref, bf16[1024,1024]{1,0:T(8,128)(2,1)S(1)} %copy-done.2), custom_call_target="tpu_custom_call" | custom-call | flops 1200000000 | bytes 6000000 | tf_op jit(solution)/shard_map/chosen/pallas_call | solution.py:199
  83.4 0.0 copy-start.7
  83.5 1.0 copy-done.7
  84.4 13.4 %all-to-all-done.2 = bf16[16,32,1024]{2,1,0:T(8,128)(2,1)S(1)} async-done(((bf16[16,32,1024]{2,1,0:T(8,128)(2,1)}), bf16[16,32,1024]{2,1,0:T(8,128)(2,1)S(1)}, u32[]{:S(2)}, u32[]{:S(2)}) %all-to-all-start.2) | async-done | bytes 1048608 | tf_op jit(solution)/shard_map/all_to_all | solution.py:230
  97.8 0.0 copy-start.8
  97.8 1.2 %copy-done.8 = bf16[512,1024]{1,0:T(8,128)(2,1)S(1)} copy-done((bf16[512,1024]{1,0:T(8,128)(2,1)S(1)}, bf16[512,1024]{1,0:T(8,128)(2,1)}, u32[]{:S(2)}) %copy-start.8) | copy-done | bytes 1048600
  99.1 2.0 %final.1 = (bf16[512,1024]{1,0:T(8,128)(2,1)}, bf16[512,1024]{1,0:T(8,128)(2,1)}) custom-call(bf16[512,1024]{1,0:T(8,128)(2,1)S(1)} %bitcast.8, bf16[512,1024]{1,0:T(8,128)(2,1)S(1)} %copy-done.8), custom_call_target="tpu_custom_call" | custom-call | flops 600000000 | bytes 4000000 | tf_op jit(solution)/shard_map/final/pallas_call | solution.py:231
Async XLA Ops:
  0.6 24.8 %copy-start.5 = (f32[16]{0:T(128)S(1)}, f32[16]{0:T(128)}, u32[]{:S(2)}) copy-start(f32[16]{0:T(128)} %scale_ref.2) | copy-start | bytes 196
  0.6 24.8 %copy-start = (bf16[1024,1024]{1,0:T(8,128)(2,1)S(1)}, bf16[1024,1024]{1,0:T(8,128)(2,1)}, u32[]{:S(2)}) copy-start(bf16[1024,1024]{1,0:T(8,128)(2,1)} %out_hbm.2) | copy-start | bytes 6291460
  25.4 0.7 copy-start.3
  26.1 37.7 %copy-start.4 = (f32[1024]{0:T(1024)S(1)}, f32[1024]{0:T(1024)}, u32[]{:S(2)}) copy-start(f32[1024]{0:T(1024)} %param.17) | copy-start | bytes 12292
  39.2 24.6 %copy-start.1 = (bf16[1024,1024]{1,0:T(8,128)(2,1)S(1)}, bf16[1024,1024]{1,0:T(8,128)(2,1)}, u32[]{:S(2)}) copy-start(bf16[1024,1024]{1,0:T(8,128)(2,1)} %out_hbm.3) | copy-start | bytes 6291460
  39.2 24.6 %copy-start.6 = (f32[16]{0:T(128)S(1)}, f32[16]{0:T(128)}, u32[]{:S(2)}) copy-start(f32[16]{0:T(128)} %scale_ref.3) | copy-start | bytes 196
  63.8 18.1 %copy-start.9 = (s32[8,64]{1,0:T(8,128)S(1)}, s32[8,64]{1,0:T(8,128)}, u32[]{:S(2)}) copy-start(s32[8,64]{1,0:T(8,128)} %param.12) | copy-start | bytes 6148
  76.7 5.5 %copy-start.2 = (bf16[1024,1024]{1,0:T(8,128)(2,1)S(1)}, bf16[1024,1024]{1,0:T(8,128)(2,1)}, u32[]{:S(2)}) copy-start(bf16[1024,1024]{1,0:T(8,128)(2,1)} %codebook_ref.1) | copy-start | bytes 6291460
  76.7 21.1 %all-to-all-start.2 = ((bf16[16,32,1024]{2,1,0:T(8,128)(2,1)}), bf16[16,32,1024]{2,1,0:T(8,128)(2,1)S(1)}, u32[]{:S(2)}, u32[]{:S(2)}) async-start(bf16[16,32,1024]{2,1,0:T(8,128)(2,1)} %bitcast.4), calls=%async_computation.2 | async-start | bytes 2097152 | tf_op jit(solution)/shard_map/all_to_all | solution.py:230
  83.4 1.0 copy-start.7
  97.8 1.2 %copy-start.8 = (bf16[512,1024]{1,0:T(8,128)(2,1)S(1)}, bf16[512,1024]{1,0:T(8,128)(2,1)}, u32[]{:S(2)}) copy-start(bf16[512,1024]{1,0:T(8,128)(2,1)} %copy-done.7) | copy-start | bytes 3145732
where the time goes:
time: 101 us
  blocking collectives  49.3 us (49%)
  Pallas kernels  29.3 us (29%)
  waiting for transfers between devices  13.4 us (13%)
  starting transfers between devices  5.24 us (5%)
  local copies, waits for them, and re-layouts  3.11 us (3%)
    all_to_all x1, blocking collectives, shards(): x = lax.all_to_all(frames_in, 'patch', 0, 0, tiled=True).reshape(512, D)  24.8 us
    all_to_all x1, blocking collectives, shards(): lax.all_to_all(stream.reshape(128, 8, 512), ('tm', 'patch'), 0, 0, tiled=...  24.5 us
    all_to_all x1, waiting for transfers between devices, shards(): lax.all_to_all(output.reshape(16, 32, D), 'tm', 0, 0, tiled=True)  13.4 us
    pallas_call x1, Pallas kernels, shards(): pl.pallas_call(spatial_kernel, out_shape=jax.ShapeDtypeStruct((16, 8, 8,...  13.1 us
    pallas_call x1, Pallas kernels, shards(): pl.pallas_call(temporal_kernel, out_shape=jax.ShapeDtypeStruct((512, D),...  12.9 us
    all_to_all x1, starting transfers between devices, shards(): lax.all_to_all(output.reshape(16, 32, D), 'tm', 0, 0, tiled=True)  5.24 us
    unnamed x20, local copies, waits for them, and re-layouts  2.91 us
    pallas_call x1, Pallas kernels, shards(): pl.pallas_call(final_kernel, out_shape=[jax.ShapeDtypeStruct((512, D), bf...  2.05 us
  transfers between devices with their start and end apart: 1, of which 1 were waited for; matrix products, arithmetic and copies ran while one was open for 0% of the time, Pallas kernels for 1%

commit v1 on v0

v1 whole, which is shorter than its diff:
```python
import functools
import math

import jax
import jax.numpy as jnp
from jax import lax
from jax.experimental import pallas as pl
from jax.experimental.pallas import tpu as pltpu
from jax.sharding import PartitionSpec as P

H = 16
HD = 64
D = 1024
GROUP = 256
PAIR = 128
ROWS = 256
LOG2E = math.log2(math.e)
f32 = jnp.float32
bf16 = jnp.bfloat16


def iota(shape, axis):
    return lax.broadcasted_iota(jnp.int32, shape, axis)


def same_head_mean():
    same = (iota((GROUP, GROUP), 0) // HD) == (iota((GROUP, GROUP), 1) // HD)
    return jnp.where(same, f32(1.0 / HD), f32(0.0)).astype(bf16)


def norm_rows(wide, gain):
    mean = jnp.mean(wide * wide, -1, keepdims=True)
    return (wide * lax.rsqrt(mean + 1e-5) * gain).astype(bf16)


def head_norm(block, averager):
    square = (block * block).astype(bf16)
    mean = jnp.dot(square, averager, preferred_element_type=f32)
    return block * lax.rsqrt(mean + 1e-6)


def scale_row(scale_ref, first_head):
    head = iota((1, GROUP), 1) // HD
    row = jnp.full((1, GROUP), scale_ref[first_head], f32)
    for h in range(1, GROUP // HD):
        row = jnp.where(head == h, scale_ref[first_head + h], row)
    return row * f32(LOG2E / HD)


def key_pair(key):
    low = iota(key.shape, 1) < HD
    zero = jnp.zeros_like(key)
    return jnp.concatenate([jnp.where(low, key, zero), jnp.where(low, zero, key)], 0)


def value_pair(value):
    low = iota(value.shape, 1) < HD
    zero = jnp.zeros_like(value)
    one = jnp.ones_like(value)
    first = jnp.concatenate([jnp.where(low, value, zero), jnp.where(low, one, zero)], 1)
    second = jnp.concatenate([jnp.where(low, zero, value), jnp.where(low, zero, one)], 1)
    return jnp.concatenate([first, second], 0)


def weight_copies(qkv_hbm, qkv_buf, sems):
    return [
        [
            pltpu.make_async_copy(
                qkv_hbm.at[:, pl.ds(part * D + g * GROUP, GROUP)],
                qkv_buf.at[:, pl.ds(part * D + g * GROUP, GROUP)],
                sems.at[part, g],
            )
            for part in range(3)
        ]
        for g in range(D // GROUP)
    ]


def row_copies(source, target, sems, count):
    return [
        pltpu.make_async_copy(source.at[pl.ds(n * count, count)], target.at[pl.ds(n * count, count)], sems.at[n])
        for n in range(source.shape[0] // count)
    ]


def project(normed, qkv, scale_ref, averager, g):
    q, k, v = (
        jnp.dot(normed, qkv[:, part * D + g * GROUP : part * D + (g + 1) * GROUP], preferred_element_type=f32)
        for part in range(3)
    )
    q = (head_norm(q, averager) * scale_row(scale_ref, 4 * g)).astype(bf16)
    return q, head_norm(k, averager).astype(bf16), v.astype(bf16)


def weighted_mean(weights, values):
    o = jnp.dot(weights, values, preferred_element_type=f32)
    return (o[:, :PAIR] / o[:, PAIR:]).astype(bf16)


def logits(q, unit):
    lanes, rows, keys, _ = unit
    return lax.dot_general(q[rows, lanes], keys, (((1,), (1,)), ((), ())), preferred_element_type=f32)


def spatial_kernel(
    x_hbm, gain_hbm, scale_ref, qkv_hbm, out_hbm, o_hbm,
    x, gain, qkv_buf, out_buf, normed, attn, o, x_sems, gain_sem, sems, out_sem, o_sems,
):
    x_copies = row_copies(x_hbm, x, x_sems, 128)
    gain_copy = pltpu.make_async_copy(gain_hbm, gain, gain_sem)
    copies = weight_copies(qkv_hbm, qkv_buf, sems)
    out_copy = pltpu.make_async_copy(out_hbm, out_buf, out_sem)
    gain_copy.start()
    for copy in x_copies + copies[0]:
        copy.start()
    gain_copy.wait()
    for n, copy in enumerate(x_copies):
        copy.wait()
        rows = slice(128 * n, 128 * (n + 1))
        normed[rows, :] = norm_rows(x[rows, :].astype(f32), gain[...])
    averager = same_head_mean()
    for g in range(4):
        for copy in copies[g]:
            copy.wait()
        for copy in copies[g + 1] if g < 3 else [out_copy]:
            copy.start()
        q, k, v = project(normed[...], qkv_buf, scale_ref, averager, g)
        units = []
        for pair in range(2):
            lanes = slice(pair * PAIR, (pair + 1) * PAIR)
            keys = key_pair(k[:, lanes])
            values = value_pair(v[:, lanes])
            for r in range(0, 512, ROWS):
                units.append((lanes, slice(r, r + ROWS), keys, values))
        s = logits(q, units[0])
        for n, (lanes, rows, keys, values) in enumerate(units):
            later = logits(q, units[n + 1]) if n + 1 < len(units) else None
            w = jnp.exp2(s).astype(bf16)
            ratio = weighted_mean(w, values)
            attn[rows, g * GROUP + lanes.start : g * GROUP + lanes.stop] = ratio
            s = later
    out_copy.wait()
    half = D // 2
    low = iota((1, 8, half), 1) < 4
    stores = []
    for n in range(2):
        rows = slice(256 * n, 256 * (n + 1))
        stream = x[rows, :].astype(f32) + jnp.dot(attn[rows, :], out_buf[...], preferred_element_type=f32)
        a = stream[:, :half].reshape(32, 8, half)
        b = stream[:, half:].reshape(32, 8, half)
        even = jnp.where(low, a, pltpu.roll(b, 4, 1)).astype(bf16)
        odd = jnp.where(low, pltpu.roll(a, 4, 1), b).astype(bf16)
        for j in range(4):
            runs = jnp.stack([even[8 * j : 8 * j + 8], odd[8 * j : 8 * j + 8]], 1)
            o[:, 4 * n + j] = runs.reshape(16, 8, half)
        store = pltpu.make_async_copy(o.at[:, pl.ds(4 * n, 4)], o_hbm.at[:, pl.ds(4 * n, 4)], o_sems.at[n])
        store.start()
        stores.append(store)
    for store in stores:
        store.wait()


def temporal_kernel(
    x_hbm, gain_hbm, scale_ref, qkv_hbm, out_hbm, o_hbm,
    x, gain, qkv_buf, out_buf, stream, normed, attn, o, x_sems, gain_sem, sems, out_sem, o_sems,
):
    x_copies = row_copies(x_hbm, x, x_sems, 32)
    gain_copy = pltpu.make_async_copy(gain_hbm, gain, gain_sem)
    copies = weight_copies(qkv_hbm, qkv_buf, sems)
    out_copy = pltpu.make_async_copy(out_hbm, out_buf, out_sem)
    gain_copy.start()
    for copy in x_copies + copies[0]:
        copy.start()
    half = D // 2
    one = f32(1.0)
    nil = f32(0.0)
    want = iota((128, 256), 0)
    source = (want & 31) * 8 + (want >> 5)
    first = jnp.where(iota((128, 256), 1) == source, one, nil).astype(bf16)
    second = jnp.where(iota((128, 256), 1) == source + 4, one, nil).astype(bf16)
    gain_copy.wait()
    for b, copy in enumerate(x_copies):
        copy.wait()
        recv = x[32 * b : 32 * (b + 1)].reshape(256, half)
        block = jnp.concatenate(
            [
                jnp.dot(first, recv, preferred_element_type=f32),
                jnp.dot(second, recv, preferred_element_type=f32),
            ],
            1,
        )
        ready = norm_rows(block, gain[...])
        for p in range(4):
            rows = slice(p * 128 + 32 * b, p * 128 + 32 * (b + 1))
            stream[rows, :] = block[32 * p : 32 * (p + 1)]
            normed[rows, :] = ready[32 * p : 32 * (p + 1)]
    averager = same_head_mean()
    causal = (iota((256, 256), 0) & 127) >= (iota((256, 256), 1) & 127)
    for g in range(4):
        for copy in copies[g]:
            copy.wait()
        for copy in copies[g + 1] if g < 3 else [out_copy]:
            copy.start()
        q, k, v = project(normed[...], qkv_buf, scale_ref, averager, g)
        for pair in range(2):
            lanes = slice(pair * PAIR, (pair + 1) * PAIR)
            for p in range(0, 4, 2):
                one_rows = slice(p * 128, (p + 1) * 128)
                two_rows = slice((p + 1) * 128, (p + 2) * 128)
                blank = jnp.zeros((128, PAIR), bf16)
                queries = jnp.concatenate(
                    [
                        jnp.concatenate([q[one_rows, lanes], blank], 1),
                        jnp.concatenate([blank, q[two_rows, lanes]], 1),
                    ],
                    0,
                )
                keys = jnp.concatenate([key_pair(k[one_rows, lanes]), key_pair(k[two_rows, lanes])], 1)
                s = lax.dot_general(queries, keys, (((1,), (1,)), ((), ())), preferred_element_type=f32)
                w = jnp.where(causal, jnp.exp2(s), nil).astype(bf16)
                for n, rows in enumerate((one_rows, two_rows)):
                    ratio = weighted_mean(w[n * 128 : (n + 1) * 128], value_pair(v[rows, lanes]))
                    attn[rows, g * GROUP + lanes.start : g * GROUP + lanes.stop] = ratio
    out_copy.wait()
    want = iota((256, 256), 0)
    source = (want & 3) * 64 + (want >> 2)
    move = jnp.where(iota((256, 256), 1) == source, one, nil).astype(bf16)
    stores = []
    for b in range(2):
        pick = [slice(p * 128 + 64 * b, p * 128 + 64 * (b + 1)) for p in range(4)]
        mixed = jnp.concatenate([attn[rows, :] for rows in pick], 0)
        base = jnp.concatenate([stream[rows, :] for rows in pick], 0)
        output = (base + jnp.dot(mixed, out_buf[...], preferred_element_type=f32)).astype(bf16)
        rows = pl.ds(256 * b, 256)
        o[rows, :] = jnp.dot(move, output, preferred_element_type=f32).astype(bf16)
        store = pltpu.make_async_copy(o.at[rows, :], o_hbm.at[rows, :], o_sems.at[b])
        store.start()
        stores.append(store)
    for store in stores:
        store.wait()


def chosen_kernel(codes_ref, codebook_ref, o_hbm, rows, sem):
    hot = jnp.where(codes_ref[...] == iota((512, D), 1), f32(1.0), f32(0.0)).astype(bf16)
    rows[...] = jnp.dot(hot, codebook_ref[...], preferred_element_type=f32).astype(bf16)
    store = pltpu.make_async_copy(rows, o_hbm, sem)
    store.start()
    store.wait()


def final_kernel(x_ref, chosen_hbm, enc_hbm, com_hbm, chosen, enc, com, sems):
    load = pltpu.make_async_copy(chosen_hbm, chosen, sems.at[0])
    load.start()
    stores = []
    want = iota((128, 128), 0)
    source = ((want >> 2) & 15) * 8 + (want >> 6) * 4 + (want & 3)
    move = jnp.where(iota((128, 128), 1) == source, f32(1.0), f32(0.0)).astype(bf16)
    for n in range(4):
        rows = pl.ds(n * 128, 128)
        block = x_ref[:, 8 * n : 8 * (n + 1), :].reshape(128, D)
        output = jnp.dot(move, block, preferred_element_type=f32)
        enc[rows, :] = output.astype(bf16)
        store = pltpu.make_async_copy(enc.at[rows, :], enc_hbm.at[rows, :], sems.at[1 + 2 * n])
        store.start()
        stores.append(store)
        if n == 0:
            load.wait()
        com[rows, :] = (output - chosen[rows, :].astype(f32)).astype(bf16)
        store = pltpu.make_async_copy(com.at[rows, :], com_hbm.at[rows, :], sems.at[2 + 2 * n])
        store.start()
        stores.append(store)
    for store in stores:
        store.wait()


VM = pl.BlockSpec(memory_space=pltpu.VMEM)
HBM = pl.BlockSpec(memory_space=pltpu.HBM)
SM = pl.BlockSpec(memory_space=pltpu.SMEM)


def params(limit):
    return pltpu.CompilerParams(vmem_limit_bytes=limit)


def cost(gmac, mbytes):
    return pl.CostEstimate(flops=int(2e9 * gmac), bytes_accessed=int(1e6 * mbytes), transcendentals=0)


def shards(frames_in, codes, gain_space, qkv_space, out_space, scale_space, gain_time, qkv_time, out_time, scale_time, codebook):
    x = lax.all_to_all(frames_in, "patch", 0, 0, tiled=True).reshape(512, D)
    chosen = pl.pallas_call(
        chosen_kernel,
        out_shape=jax.ShapeDtypeStruct((512, D), bf16),
        in_specs=[VM, VM],
        out_specs=HBM,
        scratch_shapes=[pltpu.VMEM((512, D), bf16), pltpu.SemaphoreType.DMA],
        compiler_params=params(20_000_000),
        cost_estimate=cost(0.6, 6),
        name="chosen",
    )(codes.reshape(512, 1), codebook)
    row = pltpu.VMEM((1, D), f32)
    tall = pltpu.VMEM((512, D), bf16)
    weights = [pltpu.VMEM((D, 3 * D), bf16), pltpu.VMEM((D, D), bf16)]
    sems = [
        pltpu.SemaphoreType.DMA((4,)),
        pltpu.SemaphoreType.DMA,
        pltpu.SemaphoreType.DMA((3, 4)),
        pltpu.SemaphoreType.DMA,
        pltpu.SemaphoreType.DMA((2,)),
    ]
    stream = pl.pallas_call(
        spatial_kernel,
        out_shape=jax.ShapeDtypeStruct((16, 8, 8, 512), bf16),
        in_specs=[HBM, HBM, SM, HBM, HBM],
        out_specs=HBM,
        scratch_shapes=[tall, row, *weights, tall, tall, pltpu.VMEM((16, 8, 8, 512), bf16), *sems],
        compiler_params=params(57_500_000),
        cost_estimate=cost(5, 10),
        name="spatial",
    )(x, gain_space.reshape(1, D), scale_space, qkv_space, out_space)
    stream = lax.all_to_all(stream.reshape(128, 8, 512), ("tm", "patch"), 0, 0, tiled=True)
    output = pl.pallas_call(
        temporal_kernel,
        out_shape=jax.ShapeDtypeStruct((512, D), bf16),
        in_specs=[HBM, HBM, SM, HBM, HBM],
        out_specs=HBM,
        scratch_shapes=[
            pltpu.VMEM((128, 8, 512), bf16), row, *weights, pltpu.VMEM((512, D), f32), tall, tall, tall, *sems,
        ],
        compiler_params=params(57_500_000),
        cost_estimate=cost(4, 10),
        name="temporal",
    )(stream, gain_time.reshape(1, D), scale_time, qkv_time, out_time)
    output = lax.all_to_all(output.reshape(16, 32, D), "tm", 0, 0, tiled=True)
    encoded, commitment = pl.pallas_call(
        final_kernel,
        out_shape=[jax.ShapeDtypeStruct((512, D), bf16)] * 2,
        in_specs=[VM, HBM],
        out_specs=[HBM, HBM],
        scratch_shapes=[pltpu.VMEM((512, D), bf16)] * 3 + [pltpu.SemaphoreType.DMA((9,))],
        input_output_aliases={1: 1},
        compiler_params=params(20_000_000),
        cost_estimate=cost(0.3, 4),
        name="final",
    )(output, chosen)
    return encoded.reshape(8, 64, D), commitment.reshape(8, 64, D)


def solution(mesh):
    rows = P("tm", "patch", None)
    return jax.shard_map(
        shards,
        mesh=mesh,
        in_specs=(rows, P("tm", "patch")) + (P(),) * 9,
        out_specs=(rows, rows),
        check_vma=False,
    )
```

time: 101 us -> 102 us (level)
  Pallas kernels: 29.3 us -> 32.8 us
  local copies, waits for them, and re-layouts: 3.11 us -> 0.21 us
    unnamed x20 -> x4, local copies, waits for them, and re-layouts: 2.91 us -> 0.01 us
    pallas_call x1, Pallas kernels: 13.1 us -> 14.1 us  [shards(): pl.pallas_call(spatial_kernel, out_shape=jax.ShapeDtypeStruct((16, 8, 8,...]
  transfers between devices with their start and end apart: 1 -> 1, of which waited for: 1 -> 1; matrix products, arithmetic and copies ran while one was open for 0% -> 0% of each run, Pallas kernels for 1% -> 2%
where the time goes in v1:
time: 102 us
  blocking collectives  49.6 us (49%)
  Pallas kernels  32.8 us (32%)
  waiting for transfers between devices  13.4 us (13%)
  starting transfers between devices  5.23 us (5%)
    all_to_all x1, blocking collectives, shards(): lax.all_to_all(stream.reshape(128, 8, 512), ('tm', 'patch'), 0, 0, tiled=...  24.9 us
    all_to_all x1, blocking collectives, shards(): x = lax.all_to_all(frames_in, 'patch', 0, 0, tiled=True).reshape(512, D)  24.7 us
    pallas_call x1, Pallas kernels, shards(): pl.pallas_call(spatial_kernel, out_shape=jax.ShapeDtypeStruct((16, 8, 8,...  14.1 us
    pallas_call x1, Pallas kernels, shards(): pl.pallas_call(temporal_kernel, out_shape=jax.ShapeDtypeStruct((512, D),...  13.6 us
    all_to_all x1, waiting for transfers between devices, shards(): output = lax.all_to_all(output.reshape(16, 32, D), 'tm', 0, 0, tiled=True)  13.4 us
    all_to_all x1, starting transfers between devices, shards(): output = lax.all_to_all(output.reshape(16, 32, D), 'tm', 0, 0, tiled=True)  5.23 us
    pallas_call x1, Pallas kernels, shards(): pl.pallas_call(final_kernel, out_shape=[jax.ShapeDtypeStruct((512, D), bf...  2.79 us
    pallas_call x1, Pallas kernels, shards(): pl.pallas_call(chosen_kernel, out_shape=jax.ShapeDtypeStruct((512, D), bf...  2.27 us
  transfers between devices with their start and end apart: 1, of which 1 were waited for; matrix products, arithmetic and copies ran while one was open for 0% of the time, Pallas kernels for 2%

profile of v1, /device:TPU:1, one launch (start us, length us, event | category | flops | bytes accessed | tf_op | source)
XLA Modules:
  0.0 102.0 jit_solution(8328528592237088771)
XLA Ops:
  0.6 24.7 %all_to_all.15 = bf16[8,64,1024]{2,1,0:T(8,128)(2,1)} all-to-all(bf16[8,64,1024]{2,1,0:T(8,128)(2,1)} %param.11), channel_id=1, replica_groups=mesh['tm'=16,'patch'=8] {'patch'}, dimensions={0} | all-to-all | bytes 2097152 | tf_op jit(solution)/shard_map/all_to_all | solution.py:290
  25.4 14.1 %spatial.1 = bf16[16,8,8,512]{3,2,1,0:T(8,128)(2,1)} custom-call(bf16[512,1024]{1,0:T(8,128)(2,1)} %bitcast.9, f32[1,1024]{1,0:T(1,128)} %bitcast.10, f32[16]{0:T(128)} %scale_ref.2, bf16[1024,3072]{1,0:T(8,128)(2,1)} %qkv_hbm.2, bf16[1024,1024]{1,0:T(8,128)(2,1)} %out_hbm.2), custom_call_target="tpu_custom_call" | custom-call | flops 10000000000 | bytes 10000000 | tf_op jit(solution)/shard_map/spatial/pallas_call | solution.py:311
  39.5 24.9 %all_to_all.16.x_hbm = bf16[128,8,512]{2,1,0:T(8,128)(2,1)} all-to-all(bf16[128,8,512]{2,1,0:T(8,128)(2,1)} %bitcast.8), channel_id=1, replica_groups=mesh['tm'=16,'patch'=8] {'tm','patch'}, dimensions={0} | all-to-all | bytes 2097152 | tf_op jit(solution)/shard_map/all_to_all | solution.py:321
  64.4 0.0 copy-start.1
  64.4 13.6 %temporal.1 = bf16[512,1024]{1,0:T(8,128)(2,1)} custom-call(bf16[128,8,512]{2,1,0:T(8,128)(2,1)} %all_to_all.16.x_hbm, f32[1,1024]{1,0:T(1,128)} %bitcast.11, f32[16]{0:T(128)} %scale_ref.3, bf16[1024,3072]{1,0:T(8,128)(2,1)} %qkv_hbm.3, bf16[1024,1024]{1,0:T(8,128)(2,1)} %out_hbm.3), custom_call_target="tpu_custom_call" | custom-call | flops 8000000000 | bytes 10000000 | tf_op jit(solution)/shard_map/temporal/pallas_call | solution.py:322
  77.9 0.0 copy-start
  78.0 5.2 %all-to-all-start.2 = ((bf16[16,32,1024]{2,1,0:T(8,128)(2,1)}), bf16[16,32,1024]{2,1,0:T(8,128)(2,1)S(1)}, u32[]{:S(2)}, u32[]{:S(2)}) async-start(bf16[16,32,1024]{2,1,0:T(8,128)(2,1)} %bitcast.7), calls=%async_computation.2 | async-start | bytes 2097152 | tf_op jit(solution)/shard_map/all_to_all | solution.py:334
  83.2 0.0 copy-done.1
  83.2 0.2 reshape.36.codes_ref
  83.4 0.0 copy-done
  83.4 2.3 %chosen.1.chosen_hbm = bf16[512,1024]{1,0:T(8,128)(2,1)} custom-call(s32[512,1]{1,0:T(8,128)S(1)} %reshape.36.codes_ref, bf16[1024,1024]{1,0:T(8,128)(2,1)S(1)} %copy-done), custom_call_target="tpu_custom_call" | custom-call | flops 1200000000 | bytes 6000000 | tf_op jit(solution)/shard_map/chosen/pallas_call | solution.py:291
  85.7 13.4 %all-to-all-done.2.x_ref = bf16[16,32,1024]{2,1,0:T(8,128)(2,1)S(1)} async-done(((bf16[16,32,1024]{2,1,0:T(8,128)(2,1)}), bf16[16,32,1024]{2,1,0:T(8,128)(2,1)S(1)}, u32[]{:S(2)}, u32[]{:S(2)}) %all-to-all-start.2) | async-done | bytes 1048608 | tf_op jit(solution)/shard_map/all_to_all | solution.py:334
  99.1 2.8 %final.1 = (bf16[512,1024]{1,0:T(8,128)(2,1)}, bf16[512,1024]{1,0:T(8,128)(2,1)}) custom-call(bf16[16,32,1024]{2,1,0:T(8,128)(2,1)S(1)} %all-to-all-done.2.x_ref, bf16[512,1024]{1,0:T(8,128)(2,1)} %chosen.1.chosen_hbm), custom_call_target="tpu_custom_call", output_to_operand_aliasing={{1}: (1, {})} | custom-call | flops 600000000 | bytes 4000000 | tf_op jit(solution)/shard_map/final/pallas_call | solution.py:335
Async XLA Ops:
  64.4 18.8 %copy-start.1 = (s32[8,64]{1,0:T(8,128)S(1)}, s32[8,64]{1,0:T(8,128)}, u32[]{:S(2)}) copy-start(s32[8,64]{1,0:T(8,128)} %param.12) | copy-start | bytes 6148
  77.9 5.5 %copy-start = (bf16[1024,1024]{1,0:T(8,128)(2,1)S(1)}, bf16[1024,1024]{1,0:T(8,128)(2,1)}, u32[]{:S(2)}) copy-start(bf16[1024,1024]{1,0:T(8,128)(2,1)} %codebook_ref.1) | copy-start | bytes 6291460
  78.0 21.1 %all-to-all-start.2 = ((bf16[16,32,1024]{2,1,0:T(8,128)(2,1)}), bf16[16,32,1024]{2,1,0:T(8,128)(2,1)S(1)}, u32[]{:S(2)}, u32[]{:S(2)}) async-start(bf16[16,32,1024]{2,1,0:T(8,128)(2,1)} %bitcast.7), calls=%async_computation.2 | async-start | bytes 2097152 | tf_op jit(solution)/shard_map/all_to_all | solution.py:334

commit v2 on v1

--- a/solution.py
+++ b/solution.py
@@ -62,27 +62,6 @@
     return jnp.concatenate([first, second], 0)
 
 
-def weight_copies(qkv_hbm, qkv_buf, sems):
-    return [
-        [
-            pltpu.make_async_copy(
-                qkv_hbm.at[:, pl.ds(part * D + g * GROUP, GROUP)],
-                qkv_buf.at[:, pl.ds(part * D + g * GROUP, GROUP)],
-                sems.at[part, g],
-            )
-            for part in range(3)
-        ]
-        for g in range(D // GROUP)
-    ]
-
-
-def row_copies(source, target, sems, count):
-    return [
-        pltpu.make_async_copy(source.at[pl.ds(n * count, count)], target.at[pl.ds(n * count, count)], sems.at[n])
-        for n in range(source.shape[0] // count)
-    ]
-
-
 def project(normed, qkv, scale_ref, averager, g):
     q, k, v = (
         jnp.dot(normed, qkv[:, part * D + g * GROUP : part * D + (g + 1) * GROUP], preferred_element_type=f32)
@@ -102,28 +81,32 @@
     return lax.dot_general(q[rows, lanes], keys, (((1,), (1,)), ((), ())), preferred_element_type=f32)
 
 
-def spatial_kernel(
-    x_hbm, gain_hbm, scale_ref, qkv_hbm, out_hbm, o_hbm,
-    x, gain, qkv_buf, out_buf, normed, attn, o, x_sems, gain_sem, sems, out_sem, o_sems,
-):
-    x_copies = row_copies(x_hbm, x, x_sems, 128)
-    gain_copy = pltpu.make_async_copy(gain_hbm, gain, gain_sem)
-    copies = weight_copies(qkv_hbm, qkv_buf, sems)
+def spatial_kernel(x, gain, scale_ref, qkv_hbm, out_hbm, o, qkv_buf, out_buf, normed, attn, sems, out_sem):
     out_copy = pltpu.make_async_copy(out_hbm, out_buf, out_sem)
-    gain_copy.start()
-    for copy in x_copies + copies[0]:
+    copies = [
+        [
+            pltpu.make_async_copy(
+                qkv_hbm.at[:, pl.ds(part * D + start, count)],
+                qkv_buf.at[:, pl.ds(part * D + start, count)],
+                sems.at[n, part],
+            )
+            for part in range(3)
+        ]
+        for n, (start, count) in enumerate(((0, GROUP), (GROUP, D - GROUP)))
+    ]
+    for copy in copies[0]:
         copy.start()
-    gain_copy.wait()
-    for n, copy in enumerate(x_copies):
-        copy.wait()
+    for n in range(4):
         rows = slice(128 * n, 128 * (n + 1))
         normed[rows, :] = norm_rows(x[rows, :].astype(f32), gain[...])
     averager = same_head_mean()
     for g in range(4):
-        for copy in copies[g]:
-            copy.wait()
-        for copy in copies[g + 1] if g < 3 else [out_copy]:
-            copy.start()
+        if g < 2:
+            for copy in copies[g]:
+                copy.wait()
+        if g == 0:
+            for copy in copies[1] + [out_copy]:
+                copy.start()
         q, k, v = project(normed[...], qkv_buf, scale_ref, averager, g)
         units = []
         for pair in range(2):
@@ -142,7 +125,6 @@
     out_copy.wait()
     half = D // 2
     low = iota((1, 8, half), 1) < 4
-    stores = []
     for n in range(2):
         rows = slice(256 * n, 256 * (n + 1))
         stream = x[rows, :].astype(f32) + jnp.dot(attn[rows, :], out_buf[...], preferred_element_type=f32)
@@ -153,24 +135,11 @@
         for j in range(4):
             runs = jnp.stack([even[8 * j : 8 * j + 8], odd[8 * j : 8 * j + 8]], 1)
             o[:, 4 * n + j] = runs.reshape(16, 8, half)
-        store = pltpu.make_async_copy(o.at[:, pl.ds(4 * n, 4)], o_hbm.at[:, pl.ds(4 * n, 4)], o_sems.at[n])
-        store.start()
-        stores.append(store)
-    for store in stores:
-        store.wait()
 
 
 def temporal_kernel(
-    x_hbm, gain_hbm, scale_ref, qkv_hbm, out_hbm, o_hbm,
-    x, gain, qkv_buf, out_buf, stream, normed, attn, o, x_sems, gain_sem, sems, out_sem, o_sems,
+    x, gain, scale_ref, qkv_buf, out_buf, o_hbm, stream, normed, attn, o, o_sems
 ):
-    x_copies = row_copies(x_hbm, x, x_sems, 32)
-    gain_copy = pltpu.make_async_copy(gain_hbm, gain, gain_sem)
-    copies = weight_copies(qkv_hbm, qkv_buf, sems)
-    out_copy = pltpu.make_async_copy(out_hbm, out_buf, out_sem)
-    gain_copy.start()
-    for copy in x_copies + copies[0]:
-        copy.start()
     half = D // 2
     one = f32(1.0)
     nil = f32(0.0)
@@ -178,9 +147,7 @@
     source = (want & 31) * 8 + (want >> 5)
     first = jnp.where(iota((128, 256), 1) == source, one, nil).astype(bf16)
     second = jnp.where(iota((128, 256), 1) == source + 4, one, nil).astype(bf16)
-    gain_copy.wait()
-    for b, copy in enumerate(x_copies):
-        copy.wait()
+    for b in range(4):
         recv = x[32 * b : 32 * (b + 1)].reshape(256, half)
         block = jnp.concatenate(
             [
@@ -197,10 +164,6 @@
     averager = same_head_mean()
     causal = (iota((256, 256), 0) & 127) >= (iota((256, 256), 1) & 127)
     for g in range(4):
-        for copy in copies[g]:
-            copy.wait()
-        for copy in copies[g + 1] if g < 3 else [out_copy]:
-            copy.start()
         q, k, v = project(normed[...], qkv_buf, scale_ref, averager, g)
         for pair in range(2):
             lanes = slice(pair * PAIR, (pair + 1) * PAIR)
@@ -221,7 +184,6 @@
                 for n, rows in enumerate((one_rows, two_rows)):
                     ratio = weighted_mean(w[n * 128 : (n + 1) * 128], value_pair(v[rows, lanes]))
                     attn[rows, g * GROUP + lanes.start : g * GROUP + lanes.stop] = ratio
-    out_copy.wait()
     want = iota((256, 256), 0)
     source = (want & 3) * 64 + (want >> 2)
     move = jnp.where(iota((256, 256), 1) == source, one, nil).astype(bf16)
@@ -298,23 +260,17 @@
         cost_estimate=cost(0.6, 6),
         name="chosen",
     )(codes.reshape(512, 1), codebook)
-    row = pltpu.VMEM((1, D), f32)
     tall = pltpu.VMEM((512, D), bf16)
-    weights = [pltpu.VMEM((D, 3 * D), bf16), pltpu.VMEM((D, D), bf16)]
-    sems = [
-        pltpu.SemaphoreType.DMA((4,)),
-        pltpu.SemaphoreType.DMA,
-        pltpu.SemaphoreType.DMA((3, 4)),
-        pltpu.SemaphoreType.DMA,
-        pltpu.SemaphoreType.DMA((2,)),
-    ]
     stream = pl.pallas_call(
         spatial_kernel,
         out_shape=jax.ShapeDtypeStruct((16, 8, 8, 512), bf16),
-        in_specs=[HBM, HBM, SM, HBM, HBM],
-        out_specs=HBM,
-        scratch_shapes=[tall, row, *weights, tall, tall, pltpu.VMEM((16, 8, 8, 512), bf16), *sems],
-        compiler_params=params(57_500_000),
+        in_specs=[VM, VM, SM, HBM, HBM],
+        out_specs=VM,
+        scratch_shapes=[
+            pltpu.VMEM((D, 3 * D), bf16), pltpu.VMEM((D, D), bf16), tall, tall,
+            pltpu.SemaphoreType.DMA((2, 3)), pltpu.SemaphoreType.DMA,
+        ],
+        compiler_params=params(52_500_000),
         cost_estimate=cost(5, 10),
         name="spatial",
     )(x, gain_space.reshape(1, D), scale_space, qkv_space, out_space)
@@ -322,12 +278,10 @@
     output = pl.pallas_call(
         temporal_kernel,
         out_shape=jax.ShapeDtypeStruct((512, D), bf16),
-        in_specs=[HBM, HBM, SM, HBM, HBM],
+        in_specs=[VM, VM, SM, VM, VM],
         out_specs=HBM,
-        scratch_shapes=[
-            pltpu.VMEM((128, 8, 512), bf16), row, *weights, pltpu.VMEM((512, D), f32), tall, tall, tall, *sems,
-        ],
-        compiler_params=params(57_500_000),
+        scratch_shapes=[pltpu.VMEM((512, D), f32), tall, tall, tall, pltpu.SemaphoreType.DMA((2,))],
+        compiler_params=params(20_000_000),
         cost_estimate=cost(4, 10),
         name="temporal",
     )(stream, gain_time.reshape(1, D), scale_time, qkv_time, out_time)

time: 102 us -> 97.3 us (0.954)
  Pallas kernels: 32.8 us -> 27.7 us
    pallas_call x1, Pallas kernels: 13.6 us -> 10.3 us  [shards(): pl.pallas_call(temporal_kernel, out_shape=jax.ShapeDtypeStruct((512, D),...]
    pallas_call x1, Pallas kernels: 14.1 us -> 12.4 us  [shards(): pl.pallas_call(spatial_kernel, out_shape=jax.ShapeDtypeStruct((16, 8, 8,...]
where the time goes in v2:
time: 97.3 us; the launch traced here: 97 us
  blocking collectives  49.4 us (51%)
  Pallas kernels  27.7 us (28%)
  waiting for transfers between devices  13.4 us (14%)
  starting transfers between devices  5.25 us (5%)
    all_to_all x1, blocking collectives, shards(): x = lax.all_to_all(frames_in, 'patch', 0, 0, tiled=True).reshape(512, D)  24.9 us
    all_to_all x1, blocking collectives, shards(): lax.all_to_all(stream.reshape(128, 8, 512), ('tm', 'patch'), 0, 0, tiled=...  24.5 us
    all_to_all x1, waiting for transfers between devices, shards(): output = lax.all_to_all(output.reshape(16, 32, D), 'tm', 0, 0, tiled=True)  13.4 us
    pallas_call x1, Pallas kernels, shards(): pl.pallas_call(spatial_kernel, out_shape=jax.ShapeDtypeStruct((16, 8, 8,...  12.4 us
    pallas_call x1, Pallas kernels, shards(): pl.pallas_call(temporal_kernel, out_shape=jax.ShapeDtypeStruct((512, D),...  10.3 us
    all_to_all x1, starting transfers between devices, shards(): output = lax.all_to_all(output.reshape(16, 32, D), 'tm', 0, 0, tiled=True)  5.25 us
    pallas_call x1, Pallas kernels, shards(): pl.pallas_call(final_kernel, out_shape=[jax.ShapeDtypeStruct((512, D), bf...  2.78 us
    pallas_call x1, Pallas kernels, shards(): pl.pallas_call(chosen_kernel, out_shape=jax.ShapeDtypeStruct((512, D), bf...  2.26 us
  transfers between devices with their start and end apart: 1, of which 1 were waited for; matrix products, arithmetic and copies ran while one was open for 0% of the time, Pallas kernels for 2%

profile of v2, /device:TPU:1, one launch (start us, length us, event | category | flops | bytes accessed | tf_op | source)
XLA Modules:
  0.0 97.0 jit_solution(14016010878871194006)
XLA Ops:
  0.6 0.0 copy-start.4
  0.6 0.0 copy-start.2
  0.6 0.0 slice-start
  0.7 24.9 %all_to_all.15 = bf16[8,64,1024]{2,1,0:T(8,128)(2,1)S(1)} all-to-all(bf16[8,64,1024]{2,1,0:T(8,128)(2,1)} %param.11), channel_id=1, replica_groups=mesh['tm'=16,'patch'=8] {'patch'}, dimensions={0} | all-to-all | bytes 2097152 | tf_op jit(solution)/shard_map/all_to_all | solution.py:252
  25.6 0.0 copy-done.4
  25.6 0.0 copy-done.2
  25.6 0.0 slice-start.1
  25.6 0.0 copy-start.3
  25.6 12.4 %spatial.1 = bf16[16,8,8,512]{3,2,1,0:T(8,128)(2,1)S(1)} custom-call(bf16[512,1024]{1,0:T(8,128)(2,1)S(1)} %bitcast.8, f32[1,1024]{1,0:T(1,128)S(1)} %bitcast.11, f32[16]{0:T(128)S(1)} %copy-done.4, bf16[1024,3072]{1,0:T(8,128)(2,1)} %qkv_hbm.1, bf16[1024,1024]{1,0:T(8,128)(2,1)} %out_hbm.1), custom_call_target="tpu_custom_call" | custom-call | flops 10000000000 | bytes 10000000 | tf_op jit(solution)/shard_map/spatial/pallas_call | solution.py:264
  38.0 0.0 copy-start
  38.0 0.0 copy-start.5
  38.0 24.5 %all_to_all.16.x = bf16[128,8,512]{2,1,0:T(8,128)(2,1)S(1)} all-to-all(bf16[128,8,512]{2,1,0:T(8,128)(2,1)S(1)} %bitcast.7), channel_id=1, replica_groups=mesh['tm'=16,'patch'=8] {'tm','patch'}, dimensions={0} | all-to-all | bytes 2097152 | tf_op jit(solution)/shard_map/all_to_all | solution.py:277
  62.5 0.0 slice-done
  62.5 0.0 slice-done.1
  62.5 0.0 copy-done.3
  62.5 0.0 copy-done
  62.5 0.0 copy-done.5
  62.6 0.0 copy-start.6
  62.6 10.3 %temporal.1 = bf16[512,1024]{1,0:T(8,128)(2,1)} custom-call(bf16[128,8,512]{2,1,0:T(8,128)(2,1)S(1)} %all_to_all.16.x, f32[1,1024]{1,0:T(1,128)S(1)} %bitcast.12, f32[16]{0:T(128)S(1)} %copy-done.5, bf16[1024,3072]{1,0:T(8,128)(2,1)S(1)} %bitcast.10, bf16[1024,1024]{1,0:T(8,128)(2,1)S(1)} %copy-done), custom_call_target="tpu_custom_call" | custom-call | flops 8000000000 | bytes 10000000 | tf_op jit(solution)/shard_map/temporal/pallas_call | solution.py:278
  72.9 0.0 copy-start.1
  72.9 5.2 %all-to-all-start.2 = ((bf16[16,32,1024]{2,1,0:T(8,128)(2,1)}), bf16[16,32,1024]{2,1,0:T(8,128)(2,1)S(1)}, u32[]{:S(2)}, u32[]{:S(2)}) async-start(bf16[16,32,1024]{2,1,0:T(8,128)(2,1)} %bitcast.4), calls=%async_computation.2 | async-start | bytes 2097152 | tf_op jit(solution)/shard_map/all_to_all | solution.py:288
  78.1 0.0 copy-done.6
  78.1 0.2 reshape.36.codes_ref
  78.4 0.0 copy-done.1
  78.4 2.3 %chosen.1.chosen_hbm = bf16[512,1024]{1,0:T(8,128)(2,1)} custom-call(s32[512,1]{1,0:T(8,128)S(1)} %reshape.36.codes_ref, bf16[1024,1024]{1,0:T(8,128)(2,1)S(1)} %copy-done.1), custom_call_target="tpu_custom_call" | custom-call | flops 1200000000 | bytes 6000000 | tf_op jit(solution)/shard_map/chosen/pallas_call | solution.py:253
  80.6 13.4 %all-to-all-done.2.x_ref = bf16[16,32,1024]{2,1,0:T(8,128)(2,1)S(1)} async-done(((bf16[16,32,1024]{2,1,0:T(8,128)(2,1)}), bf16[16,32,1024]{2,1,0:T(8,128)(2,1)S(1)}, u32[]{:S(2)}, u32[]{:S(2)}) %all-to-all-start.2) | async-done | bytes 1048608 | tf_op jit(solution)/shard_map/all_to_all | solution.py:288
  94.0 2.8 %final.1 = (bf16[512,1024]{1,0:T(8,128)(2,1)}, bf16[512,1024]{1,0:T(8,128)(2,1)}) custom-call(bf16[16,32,1024]{2,1,0:T(8,128)(2,1)S(1)} %all-to-all-done.2.x_ref, bf16[512,1024]{1,0:T(8,128)(2,1)} %chosen.1.chosen_hbm), custom_call_target="tpu_custom_call", output_to_operand_aliasing={{1}: (1, {})} | custom-call | flops 600000000 | bytes 4000000 | tf_op jit(solution)/shard_map/final/pallas_call | solution.py:289
  (1 shorter events, 0.0 us)
Async XLA Ops:
  0.6 24.9 %copy-start.4 = (f32[16]{0:T(128)S(1)}, f32[16]{0:T(128)}, u32[]{:S(2)}) copy-start(f32[16]{0:T(128)} %scale_ref.2) | copy-start | bytes 196
  0.6 24.9 %copy-start.2 = (f32[1024]{0:T(1024)S(1)}, f32[1024]{0:T(1024)}, u32[]{:S(2)}) copy-start(f32[1024]{0:T(1024)} %param.13) | copy-start | bytes 12292
  0.6 61.9 %slice-start = ((s8[6291456]{0:T(1024)(128)(4,1)}), s8[4194304]{0:T(1024)(128)(4,1)S(1)}, s32[]{:S(2)}) async-start(s8[6291456]{0:T(1024)(128)(4,1)} %bitcast.9), calls=%async_computation.3 | async-start | bytes 8388608
  25.6 37.0 %slice-start.1 = ((s8[6291456]{0:T(1024)(128)(4,1)}), s8[2097152]{0:T(1024)(128)(4,1)S(1)}, s32[]{:S(2)}) async-start(s8[6291456]{0:T(1024)(128)(4,1)} %bitcast.9), calls=%async_computation.4 | async-start | bytes 4194304
  25.6 37.0 %copy-start.3 = (f32[1024]{0:T(1024)S(1)}, f32[1024]{0:T(1024)}, u32[]{:S(2)}) copy-start(f32[1024]{0:T(1024)} %param.17) | copy-start | bytes 12292
  38.0 24.6 %copy-start = (bf16[1024,1024]{1,0:T(8,128)(2,1)S(1)}, bf16[1024,1024]{1,0:T(8,128)(2,1)}, u32[]{:S(2)}) copy-start(bf16[1024,1024]{1,0:T(8,128)(2,1)} %out_buf.1) | copy-start | bytes 6291460
  38.0 24.6 %copy-start.5 = (f32[16]{0:T(128)S(1)}, f32[16]{0:T(128)}, u32[]{:S(2)}) copy-start(f32[16]{0:T(128)} %scale_ref.3) | copy-start | bytes 196
  62.6 15.6 %copy-start.6 = (s32[8,64]{1,0:T(8,128)S(1)}, s32[8,64]{1,0:T(8,128)}, u32[]{:S(2)}) copy-start(s32[8,64]{1,0:T(8,128)} %param.12) | copy-start | bytes 6148
  72.9 5.5 %copy-start.1 = (bf16[1024,1024]{1,0:T(8,128)(2,1)S(1)}, bf16[1024,1024]{1,0:T(8,128)(2,1)}, u32[]{:S(2)}) copy-start(bf16[1024,1024]{1,0:T(8,128)(2,1)} %codebook_ref.1) | copy-start | bytes 6291460
  72.9 21.2 %all-to-all-start.2 = ((bf16[16,32,1024]{2,1,0:T(8,128)(2,1)}), bf16[16,32,1024]{2,1,0:T(8,128)(2,1)S(1)}, u32[]{:S(2)}, u32[]{:S(2)}) async-start(bf16[16,32,1024]{2,1,0:T(8,128)(2,1)} %bitcast.4), calls=%async_computation.2 | async-start | bytes 2097152 | tf_op jit(solution)/shard_map/all_to_all | solution.py:288

commit v3 on v2

--- a/solution.py
+++ b/solution.py
@@ -81,7 +81,10 @@
     return lax.dot_general(q[rows, lanes], keys, (((1,), (1,)), ((), ())), preferred_element_type=f32)
 
 
-def spatial_kernel(x, gain, scale_ref, qkv_hbm, out_hbm, o, qkv_buf, out_buf, normed, attn, sems, out_sem):
+def spatial_kernel(
+    x, gain, scale_ref, codes, codebook, qkv_hbm, out_hbm, o, chosen_hbm,
+    qkv_buf, out_buf, chosen, normed, attn, sems, out_sem, chosen_sem,
+):
     out_copy = pltpu.make_async_copy(out_hbm, out_buf, out_sem)
     copies = [
         [
@@ -96,6 +99,13 @@
     ]
     for copy in copies[0]:
         copy.start()
+    turned = codes[...].astype(f32).T
+    for f in range(8):
+        hot = jnp.where(turned[:, f : f + 1].astype(jnp.int32) == iota((64, D), 1), f32(1.0), f32(0.0)).astype(bf16)
+        normed[64 * f : 64 * (f + 1), :] = hot
+    chosen[...] = jnp.dot(normed[...], codebook[...], preferred_element_type=f32).astype(bf16)
+    chosen_copy = pltpu.make_async_copy(chosen, chosen_hbm, chosen_sem)
+    chosen_copy.start()
     for n in range(4):
         rows = slice(128 * n, 128 * (n + 1))
         normed[rows, :] = norm_rows(x[rows, :].astype(f32), gain[...])
@@ -135,6 +145,7 @@
         for j in range(4):
             runs = jnp.stack([even[8 * j : 8 * j + 8], odd[8 * j : 8 * j + 8]], 1)
             o[:, 4 * n + j] = runs.reshape(16, 8, half)
+    chosen_copy.wait()
 
 
 def temporal_kernel(
@@ -202,14 +213,6 @@
         store.wait()
 
 
-def chosen_kernel(codes_ref, codebook_ref, o_hbm, rows, sem):
-    hot = jnp.where(codes_ref[...] == iota((512, D), 1), f32(1.0), f32(0.0)).astype(bf16)
-    rows[...] = jnp.dot(hot, codebook_ref[...], preferred_element_type=f32).astype(bf16)
-    store = pltpu.make_async_copy(rows, o_hbm, sem)
-    store.start()
-    store.wait()
-
-
 def final_kernel(x_ref, chosen_hbm, enc_hbm, com_hbm, chosen, enc, com, sems):
     load = pltpu.make_async_copy(chosen_hbm, chosen, sems.at[0])
     load.start()
@@ -217,18 +220,21 @@
     want = iota((128, 128), 0)
     source = ((want >> 2) & 15) * 8 + (want >> 6) * 4 + (want & 3)
     move = jnp.where(iota((128, 128), 1) == source, f32(1.0), f32(0.0)).astype(bf16)
+    outputs = []
     for n in range(4):
         rows = pl.ds(n * 128, 128)
         block = x_ref[:, 8 * n : 8 * (n + 1), :].reshape(128, D)
         output = jnp.dot(move, block, preferred_element_type=f32)
+        outputs.append(output)
         enc[rows, :] = output.astype(bf16)
-        store = pltpu.make_async_copy(enc.at[rows, :], enc_hbm.at[rows, :], sems.at[1 + 2 * n])
+        store = pltpu.make_async_copy(enc.at[rows, :], enc_hbm.at[rows, :], sems.at[1 + n])
         store.start()
         stores.append(store)
-        if n == 0:
-            load.wait()
+    load.wait()
+    for n, output in enumerate(outputs):
+        rows = pl.ds(n * 128, 128)
         com[rows, :] = (output - chosen[rows, :].astype(f32)).astype(bf16)
-        store = pltpu.make_async_copy(com.at[rows, :], com_hbm.at[rows, :], sems.at[2 + 2 * n])
+        store = pltpu.make_async_copy(com.at[rows, :], com_hbm.at[rows, :], sems.at[5 + n])
         store.start()
         stores.append(store)
     for store in stores:
@@ -250,30 +256,20 @@
 
 def shards(frames_in, codes, gain_space, qkv_space, out_space, scale_space, gain_time, qkv_time, out_time, scale_time, codebook):
     x = lax.all_to_all(frames_in, "patch", 0, 0, tiled=True).reshape(512, D)
-    chosen = pl.pallas_call(
-        chosen_kernel,
-        out_shape=jax.ShapeDtypeStruct((512, D), bf16),
-        in_specs=[VM, VM],
-        out_specs=HBM,
-        scratch_shapes=[pltpu.VMEM((512, D), bf16), pltpu.SemaphoreType.DMA],
-        compiler_params=params(20_000_000),
-        cost_estimate=cost(0.6, 6),
-        name="chosen",
-    )(codes.reshape(512, 1), codebook)
     tall = pltpu.VMEM((512, D), bf16)
-    stream = pl.pallas_call(
+    stream, chosen = pl.pallas_call(
         spatial_kernel,
-        out_shape=jax.ShapeDtypeStruct((16, 8, 8, 512), bf16),
-        in_specs=[VM, VM, SM, HBM, HBM],
-        out_specs=VM,
+        out_shape=[jax.ShapeDtypeStruct((16, 8, 8, 512), bf16), jax.ShapeDtypeStruct((512, D), bf16)],
+        in_specs=[VM, VM, SM, VM, VM, HBM, HBM],
+        out_specs=[VM, HBM],
         scratch_shapes=[
-            pltpu.VMEM((D, 3 * D), bf16), pltpu.VMEM((D, D), bf16), tall, tall,
-            pltpu.SemaphoreType.DMA((2, 3)), pltpu.SemaphoreType.DMA,
+            pltpu.VMEM((D, 3 * D), bf16), pltpu.VMEM((D, D), bf16), tall, tall, tall,
+            pltpu.SemaphoreType.DMA((2, 3)), pltpu.SemaphoreType.DMA, pltpu.SemaphoreType.DMA,
         ],
-        compiler_params=params(52_500_000),
+        compiler_params=params(51_500_000),
         cost_estimate=cost(5, 10),
         name="spatial",
-    )(x, gain_space.reshape(1, D), scale_space, qkv_space, out_space)
+    )(x, gain_space.reshape(1, D), scale_space, codes, codebook, qkv_space, out_space)
     stream = lax.all_to_all(stream.reshape(128, 8, 512), ("tm", "patch"), 0, 0, tiled=True)
     output = pl.pallas_call(
         temporal_kernel,

time: 97.3 us -> 97.7 us (level)
  blocking collectives: 49.4 us -> 69.6 us
  waiting for transfers between devices: 13.4 us -> 0 us
  starting transfers between devices: 5.25 us -> 0 us
  Pallas kernels: 27.7 us -> 25.2 us
  local copies, waits for them, and re-layouts: 0.25 us -> 1.74 us
    all_to_all x0 -> x1, blocking collectives: none -> 20.3 us  [shards(): output = lax.all_to_all(output.reshape(16, 32, D), 'tm', 0, 0, tiled=True)]
    all_to_all x1 -> x0, waiting for transfers between devices: 13.4 us -> none  [shards(): output = lax.all_to_all(output.reshape(16, 32, D), 'tm', 0, 0, tiled=True)]
    all_to_all x1 -> x0, starting transfers between devices: 5.25 us -> none  [shards(): output = lax.all_to_all(output.reshape(16, 32, D), 'tm', 0, 0, tiled=True)]
    pallas_call x2 -> x1, Pallas kernels: 14.6 us -> 12.9 us  [shards(): pl.pallas_call(spatial_kernel, out_shape=[jax.ShapeDtypeStruct((16, 8, 8,...]
    unnamed x18, local copies, waits for them, and re-layouts: 0.05 us -> 1.74 us
  transfers between devices with their start and end apart: 1 -> 0, of which waited for: 1 -> 0; matrix products, arithmetic and copies ran while one was open for 0% -> 0% of each run, Pallas kernels for 2% -> 0%
where the time goes in v3:
time: 97.7 us; the launch traced here: 97.5 us
  blocking collectives  69.6 us (71%)
  Pallas kernels  25.2 us (26%)
  local copies, waits for them, and re-layouts  1.74 us (2%)
    all_to_all x1, blocking collectives, shards(): x = lax.all_to_all(frames_in, 'patch', 0, 0, tiled=True).reshape(512, D)  24.8 us
    all_to_all x1, blocking collectives, shards(): lax.all_to_all(stream.reshape(128, 8, 512), ('tm', 'patch'), 0, 0, tiled=...  24.5 us
    all_to_all x1, blocking collectives, shards(): output = lax.all_to_all(output.reshape(16, 32, D), 'tm', 0, 0, tiled=True)  20.3 us
    pallas_call x1, Pallas kernels, shards(): pl.pallas_call(spatial_kernel, out_shape=[jax.ShapeDtypeStruct((16, 8, 8,...  12.9 us
    pallas_call x1, Pallas kernels, shards(): pl.pallas_call(temporal_kernel, out_shape=jax.ShapeDtypeStruct((512, D),...  9.84 us
    pallas_call x1, Pallas kernels, shards(): pl.pallas_call(final_kernel, out_shape=[jax.ShapeDtypeStruct((512, D), bf...  2.5 us

profile of v3, /device:TPU:1, one launch (start us, length us, event | category | flops | bytes accessed | tf_op | source)
XLA Modules:
  0.0 97.5 jit_solution(11710811823484738389)
XLA Ops:
  0.6 0.0 copy-start
  0.6 0.0 copy-start.5
  0.6 24.8 %all_to_all.15 = bf16[8,64,1024]{2,1,0:T(8,128)(2,1)S(1)} all-to-all(bf16[8,64,1024]{2,1,0:T(8,128)(2,1)} %param.11), channel_id=1, replica_groups=mesh['tm'=16,'patch'=8] {'patch'}, dimensions={0} | all-to-all | bytes 2097152 | tf_op jit(solution)/shard_map/all_to_all | solution.py:258
  25.4 0.0 slice-start
  25.4 0.0 copy-done
  25.4 0.0 copy-done.5
  25.4 0.0 copy-start.2
  25.4 0.8 copy-done.2
  26.3 0.0 copy-start.3
  26.3 0.9 copy-done.3
  27.1 0.0 slice-start.1
  27.1 12.9 %spatial.1 = (bf16[16,8,8,512]{3,2,1,0:T(8,128)(2,1)S(1)}, bf16[512,1024]{1,0:T(8,128)(2,1)}) custom-call(bf16[512,1024]{1,0:T(8,128)(2,1)S(1)} %bitcast.8, f32[1,1024]{1,0:T(1,128)S(1)} %bitcast.12, f32[16]{0:T(128)S(1)} %copy-done.5, s32[8,64]{1,0:T(8,128)S(1)} %copy-done.3, bf16[1024,1024]{1,0:T(8,128)(2,1)S(1)} %copy-done, bf16[1024,3072]{1,0:T(8,128)(2,1)} %qkv_hbm.1, ...), custom_call_target="tpu_custom_call" | custom-call | flops 10000000000 | bytes 10000000 | tf_op jit(solution)/shard_map/spatial/pallas_call | solution.py:260
  40.0 0.0 copy-start.1
  40.0 0.0 copy-start.4
  40.1 0.0 copy-start.6
  40.1 24.5 %all_to_all.16.x = bf16[128,8,512]{2,1,0:T(8,128)(2,1)S(1)} all-to-all(bf16[128,8,512]{2,1,0:T(8,128)(2,1)S(1)} %bitcast.7), channel_id=1, replica_groups=mesh['tm'=16,'patch'=8] {'tm','patch'}, dimensions={0} | all-to-all | bytes 2097152 | tf_op jit(solution)/shard_map/all_to_all | solution.py:273
  64.6 0.0 slice-done
  64.6 0.0 slice-done.1
  64.6 0.0 copy-done.1
  64.6 0.0 copy-done.4
  64.6 0.0 copy-done.6
  64.7 9.8 %temporal.1 = bf16[512,1024]{1,0:T(8,128)(2,1)S(1)} custom-call(bf16[128,8,512]{2,1,0:T(8,128)(2,1)S(1)} %all_to_all.16.x, f32[1,1024]{1,0:T(1,128)S(1)} %bitcast.13, f32[16]{0:T(128)S(1)} %copy-done.6, bf16[1024,3072]{1,0:T(8,128)(2,1)S(1)} %bitcast.11, bf16[1024,1024]{1,0:T(8,128)(2,1)S(1)} %copy-done.1), custom_call_target="tpu_custom_call" | custom-call | flops 8000000000 | bytes 10000000 | tf_op jit(solution)/shard_map/temporal/pallas_call | solution.py:274
  74.5 20.3 %all_to_all.17.x_ref = bf16[16,32,1024]{2,1,0:T(8,128)(2,1)S(1)} all-to-all(bf16[16,32,1024]{2,1,0:T(8,128)(2,1)S(1)} %bitcast.9), channel_id=1, replica_groups=mesh['tm'=16,'patch'=8] {'tm'}, dimensions={0} | all-to-all | bytes 2097152 | tf_op jit(solution)/shard_map/all_to_all | solution.py:284
  94.8 2.5 %final.1 = (bf16[512,1024]{1,0:T(8,128)(2,1)}, bf16[512,1024]{1,0:T(8,128)(2,1)}) custom-call(bf16[16,32,1024]{2,1,0:T(8,128)(2,1)S(1)} %all_to_all.17.x_ref, bf16[512,1024]{1,0:T(8,128)(2,1)} %get-tuple-element.7.chosen_hbm), custom_call_target="tpu_custom_call", output_to_operand_aliasing={{1}: (1, {})} | custom-call | flops 600000000 | bytes 4000000 | tf_op jit(solution)/shard_map/final/pallas_call | solution.py:285
  (1 shorter events, 0.0 us)
Async XLA Ops:
  0.6 24.8 %copy-start = (bf16[1024,1024]{1,0:T(8,128)(2,1)S(1)}, bf16[1024,1024]{1,0:T(8,128)(2,1)}, u32[]{:S(2)}) copy-start(bf16[1024,1024]{1,0:T(8,128)(2,1)} %codebook.1) | copy-start | bytes 6291460
  0.6 24.8 %copy-start.5 = (f32[16]{0:T(128)S(1)}, f32[16]{0:T(128)}, u32[]{:S(2)}) copy-start(f32[16]{0:T(128)} %scale_ref.2) | copy-start | bytes 196
  25.4 39.2 %slice-start = ((s8[6291456]{0:T(1024)(128)(4,1)}), s8[4194304]{0:T(1024)(128)(4,1)S(1)}, s32[]{:S(2)}) async-start(s8[6291456]{0:T(1024)(128)(4,1)} %bitcast.10), calls=%async_computation.3 | async-start | bytes 8388608
  25.4 0.8 copy-start.2
  26.3 0.9 copy-start.3
  27.1 37.5 %slice-start.1 = ((s8[6291456]{0:T(1024)(128)(4,1)}), s8[2097152]{0:T(1024)(128)(4,1)S(1)}, s32[]{:S(2)}) async-start(s8[6291456]{0:T(1024)(128)(4,1)} %bitcast.10), calls=%async_computation.4 | async-start | bytes 4194304
  40.0 24.6 %copy-start.1 = (bf16[1024,1024]{1,0:T(8,128)(2,1)S(1)}, bf16[1024,1024]{1,0:T(8,128)(2,1)}, u32[]{:S(2)}) copy-start(bf16[1024,1024]{1,0:T(8,128)(2,1)} %out_buf.1) | copy-start | bytes 6291460
  40.0 24.6 %copy-start.4 = (f32[1024]{0:T(1024)S(1)}, f32[1024]{0:T(1024)}, u32[]{:S(2)}) copy-start(f32[1024]{0:T(1024)} %param.17) | copy-start | bytes 12292
  40.1 24.6 %copy-start.6 = (f32[16]{0:T(128)S(1)}, f32[16]{0:T(128)}, u32[]{:S(2)}) copy-start(f32[16]{0:T(128)} %scale_ref.3) | copy-start | bytes 196

commit v4 on v3

--- a/solution.py
+++ b/solution.py
@@ -82,8 +82,7 @@
 
 
 def spatial_kernel(
-    x, gain, scale_ref, codes, codebook, qkv_hbm, out_hbm, o, chosen_hbm,
-    qkv_buf, out_buf, chosen, normed, attn, sems, out_sem, chosen_sem,
+    x, gain, scale_ref, qkv_hbm, out_hbm, o, qkv_buf, out_buf, normed, attn, sems, out_sem
 ):
     out_copy = pltpu.make_async_copy(out_hbm, out_buf, out_sem)
     copies = [
@@ -99,13 +98,6 @@
     ]
     for copy in copies[0]:
         copy.start()
-    turned = codes[...].astype(f32).T
-    for f in range(8):
-        hot = jnp.where(turned[:, f : f + 1].astype(jnp.int32) == iota((64, D), 1), f32(1.0), f32(0.0)).astype(bf16)
-        normed[64 * f : 64 * (f + 1), :] = hot
-    chosen[...] = jnp.dot(normed[...], codebook[...], preferred_element_type=f32).astype(bf16)
-    chosen_copy = pltpu.make_async_copy(chosen, chosen_hbm, chosen_sem)
-    chosen_copy.start()
     for n in range(4):
         rows = slice(128 * n, 128 * (n + 1))
         normed[rows, :] = norm_rows(x[rows, :].astype(f32), gain[...])
@@ -145,12 +137,19 @@
         for j in range(4):
             runs = jnp.stack([even[8 * j : 8 * j + 8], odd[8 * j : 8 * j + 8]], 1)
             o[:, 4 * n + j] = runs.reshape(16, 8, half)
-    chosen_copy.wait()
 
 
 def temporal_kernel(
-    x, gain, scale_ref, qkv_buf, out_buf, o_hbm, stream, normed, attn, o, o_sems
+    x, gain, scale_ref, qkv_buf, out_buf, codes, codebook, o_hbm, chosen_hbm,
+    stream, normed, attn, o, chosen, o_sems, chosen_sem,
 ):
+    turned = codes[...].astype(f32).T
+    for f in range(8):
+        hot = jnp.where(turned[:, f : f + 1].astype(jnp.int32) == iota((64, D), 1), f32(1.0), f32(0.0)).astype(bf16)
+        attn[64 * f : 64 * (f + 1), :] = hot
+    chosen[...] = jnp.dot(attn[...], codebook[...], preferred_element_type=f32).astype(bf16)
+    chosen_copy = pltpu.make_async_copy(chosen, chosen_hbm, chosen_sem)
+    chosen_copy.start()
     half = D // 2
     one = f32(1.0)
     nil = f32(0.0)
@@ -211,6 +210,7 @@
         stores.append(store)
     for store in stores:
         store.wait()
+    chosen_copy.wait()
 
 
 def final_kernel(x_ref, chosen_hbm, enc_hbm, com_hbm, chosen, enc, com, sems):
@@ -257,30 +257,33 @@
 def shards(frames_in, codes, gain_space, qkv_space, out_space, scale_space, gain_time, qkv_time, out_time, scale_time, codebook):
     x = lax.all_to_all(frames_in, "patch", 0, 0, tiled=True).reshape(512, D)
     tall = pltpu.VMEM((512, D), bf16)
-    stream, chosen = pl.pallas_call(
+    stream = pl.pallas_call(
         spatial_kernel,
-        out_shape=[jax.ShapeDtypeStruct((16, 8, 8, 512), bf16), jax.ShapeDtypeStruct((512, D), bf16)],
-        in_specs=[VM, VM, SM, VM, VM, HBM, HBM],
-        out_specs=[VM, HBM],
+        out_shape=jax.ShapeDtypeStruct((16, 8, 8, 512), bf16),
+        in_specs=[VM, VM, SM, HBM, HBM],
+        out_specs=VM,
         scratch_shapes=[
-            pltpu.VMEM((D, 3 * D), bf16), pltpu.VMEM((D, D), bf16), tall, tall, tall,
-            pltpu.SemaphoreType.DMA((2, 3)), pltpu.SemaphoreType.DMA, pltpu.SemaphoreType.DMA,
+            pltpu.VMEM((D, 3 * D), bf16), pltpu.VMEM((D, D), bf16), tall, tall,
+            pltpu.SemaphoreType.DMA((2, 3)), pltpu.SemaphoreType.DMA,
         ],
-        compiler_params=params(51_500_000),
+        compiler_params=params(52_500_000),
         cost_estimate=cost(5, 10),
         name="spatial",
-    )(x, gain_space.reshape(1, D), scale_space, codes, codebook, qkv_space, out_space)
+    )(x, gain_space.reshape(1, D), scale_space, qkv_space, out_space)
     stream = lax.all_to_all(stream.reshape(128, 8, 512), ("tm", "patch"), 0, 0, tiled=True)
-    output = pl.pallas_call(
+    output, chosen = pl.pallas_call(
         temporal_kernel,
-        out_shape=jax.ShapeDtypeStruct((512, D), bf16),
-        in_specs=[VM, VM, SM, VM, VM],
-        out_specs=HBM,
-        scratch_shapes=[pltpu.VMEM((512, D), f32), tall, tall, tall, pltpu.SemaphoreType.DMA((2,))],
+        out_shape=[jax.ShapeDtypeStruct((512, D), bf16)] * 2,
+        in_specs=[VM, VM, SM, VM, VM, VM, VM],
+        out_specs=[HBM, HBM],
+        scratch_shapes=[
+            pltpu.VMEM((512, D), f32), tall, tall, tall, tall,
+            pltpu.SemaphoreType.DMA((2,)), pltpu.SemaphoreType.DMA,
+        ],
         compiler_params=params(20_000_000),
         cost_estimate=cost(4, 10),
         name="temporal",
-    )(stream, gain_time.reshape(1, D), scale_time, qkv_time, out_time)
+    )(stream, gain_time.reshape(1, D), scale_time, qkv_time, out_time, codes, codebook)
     output = lax.all_to_all(output.reshape(16, 32, D), "tm", 0, 0, tiled=True)
     encoded, commitment = pl.pallas_call(
         final_kernel,

time: 97.7 us -> 97.1 us (level)
  local copies, waits for them, and re-layouts: 1.74 us -> 0.05 us
    unnamed x18, local copies, waits for them, and re-layouts: 1.74 us -> 0.05 us
where the time goes in v4:
time: 97.1 us; the launch traced here: 96.9 us
  blocking collectives  69.7 us (72%)
  Pallas kernels  26.1 us (27%)
    all_to_all x1, blocking collectives, shards(): x = lax.all_to_all(frames_in, 'patch', 0, 0, tiled=True).reshape(512, D)  24.9 us
    all_to_all x1, blocking collectives, shards(): lax.all_to_all(stream.reshape(128, 8, 512), ('tm', 'patch'), 0, 0, tiled=...  24.5 us
    all_to_all x1, blocking collectives, shards(): output = lax.all_to_all(output.reshape(16, 32, D), 'tm', 0, 0, tiled=True)  20.3 us
    pallas_call x1, Pallas kernels, shards(): pl.pallas_call(spatial_kernel, out_shape=jax.ShapeDtypeStruct((16, 8, 8,...  12.6 us
    pallas_call x1, Pallas kernels, shards(): pl.pallas_call(temporal_kernel, out_shape=[jax.ShapeDtypeStruct((512, D),...  11.1 us
    pallas_call x1, Pallas kernels, shards(): pl.pallas_call(final_kernel, out_shape=[jax.ShapeDtypeStruct((512, D), bf...  2.52 us

profile of v4, /device:TPU:1, one launch (start us, length us, event | category | flops | bytes accessed | tf_op | source)
XLA Modules:
  0.0 96.9 jit_solution(1318650288685820851)
XLA Ops:
  0.6 0.0 copy-start.5
  0.6 0.0 copy-start.2
  0.6 0.0 slice-start
  0.7 24.9 %all_to_all.15 = bf16[8,64,1024]{2,1,0:T(8,128)(2,1)S(1)} all-to-all(bf16[8,64,1024]{2,1,0:T(8,128)(2,1)} %param.11), channel_id=1, replica_groups=mesh['tm'=16,'patch'=8] {'patch'}, dimensions={0} | all-to-all | bytes 2097152 | tf_op jit(solution)/shard_map/all_to_all | solution.py:258
  25.6 0.0 copy-done.5
  25.6 0.0 copy-done.2
  25.6 0.0 slice-start.1
  25.6 0.0 copy-start.1
  25.6 0.0 copy-start.3
  25.6 0.0 copy-start.4
  25.6 12.6 %spatial.1 = bf16[16,8,8,512]{3,2,1,0:T(8,128)(2,1)S(1)} custom-call(bf16[512,1024]{1,0:T(8,128)(2,1)S(1)} %bitcast.9, f32[1,1024]{1,0:T(1,128)S(1)} %bitcast.12, f32[16]{0:T(128)S(1)} %copy-done.5, bf16[1024,3072]{1,0:T(8,128)(2,1)} %qkv_hbm.1, bf16[1024,1024]{1,0:T(8,128)(2,1)} %out_hbm.1), custom_call_target="tpu_custom_call" | custom-call | flops 10000000000 | bytes 10000000 | tf_op jit(solution)/shard_map/spatial/pallas_call | solution.py:260
  38.2 0.0 copy-start
  38.2 0.0 copy-start.6
  38.2 24.5 %all_to_all.16.x = bf16[128,8,512]{2,1,0:T(8,128)(2,1)S(1)} all-to-all(bf16[128,8,512]{2,1,0:T(8,128)(2,1)S(1)} %bitcast.8), channel_id=1, replica_groups=mesh['tm'=16,'patch'=8] {'tm','patch'}, dimensions={0} | all-to-all | bytes 2097152 | tf_op jit(solution)/shard_map/all_to_all | solution.py:273
  62.7 0.0 slice-done
  62.7 0.0 slice-done.1
  62.7 0.0 copy-done.1
  62.7 0.0 copy-done.3
  62.8 0.0 copy-done.4
  62.8 0.0 copy-done
  62.8 0.0 copy-done.6
  62.8 11.1 %temporal.1 = (bf16[512,1024]{1,0:T(8,128)(2,1)S(1)}, bf16[512,1024]{1,0:T(8,128)(2,1)}) custom-call(bf16[128,8,512]{2,1,0:T(8,128)(2,1)S(1)} %all_to_all.16.x, f32[1,1024]{1,0:T(1,128)S(1)} %bitcast.13, f32[16]{0:T(128)S(1)} %copy-done.6, bf16[1024,3072]{1,0:T(8,128)(2,1)S(1)} %bitcast.11, bf16[1024,1024]{1,0:T(8,128)(2,1)S(1)} %copy-done, ...), custom_call_target="tpu_custom_call" | custom-call | flops 8000000000 | bytes 10000000 | tf_op jit(solution)/shard_map/temporal/pallas_call | solution.py:274
  73.9 20.3 %all_to_all.17.x_ref = bf16[16,32,1024]{2,1,0:T(8,128)(2,1)S(1)} all-to-all(bf16[16,32,1024]{2,1,0:T(8,128)(2,1)S(1)} %bitcast.7), channel_id=1, replica_groups=mesh['tm'=16,'patch'=8] {'tm'}, dimensions={0} | all-to-all | bytes 2097152 | tf_op jit(solution)/shard_map/all_to_all | solution.py:287
  94.2 2.5 %final.1 = (bf16[512,1024]{1,0:T(8,128)(2,1)}, bf16[512,1024]{1,0:T(8,128)(2,1)}) custom-call(bf16[16,32,1024]{2,1,0:T(8,128)(2,1)S(1)} %all_to_all.17.x_ref, bf16[512,1024]{1,0:T(8,128)(2,1)} %get-tuple-element.7.chosen_hbm), custom_call_target="tpu_custom_call", output_to_operand_aliasing={{1}: (1, {})} | custom-call | flops 600000000 | bytes 4000000 | tf_op jit(solution)/shard_map/final/pallas_call | solution.py:288
  (1 shorter events, 0.0 us)
Async XLA Ops:
  0.6 24.9 %copy-start.5 = (f32[16]{0:T(128)S(1)}, f32[16]{0:T(128)}, u32[]{:S(2)}) copy-start(f32[16]{0:T(128)} %scale_ref.2) | copy-start | bytes 196
  0.6 24.9 %copy-start.2 = (f32[1024]{0:T(1024)S(1)}, f32[1024]{0:T(1024)}, u32[]{:S(2)}) copy-start(f32[1024]{0:T(1024)} %param.13) | copy-start | bytes 12292
  0.6 62.1 %slice-start = ((s8[6291456]{0:T(1024)(128)(4,1)}), s8[4194304]{0:T(1024)(128)(4,1)S(1)}, s32[]{:S(2)}) async-start(s8[6291456]{0:T(1024)(128)(4,1)} %bitcast.10), calls=%async_computation.3 | async-start | bytes 8388608
  25.6 37.2 %slice-start.1 = ((s8[6291456]{0:T(1024)(128)(4,1)}), s8[2097152]{0:T(1024)(128)(4,1)S(1)}, s32[]{:S(2)}) async-start(s8[6291456]{0:T(1024)(128)(4,1)} %bitcast.10), calls=%async_computation.4 | async-start | bytes 4194304
  25.6 37.2 %copy-start.1 = (bf16[1024,1024]{1,0:T(8,128)(2,1)S(1)}, bf16[1024,1024]{1,0:T(8,128)(2,1)}, u32[]{:S(2)}) copy-start(bf16[1024,1024]{1,0:T(8,128)(2,1)} %codebook.1) | copy-start | bytes 6291460
  25.6 37.2 %copy-start.3 = (f32[1024]{0:T(1024)S(1)}, f32[1024]{0:T(1024)}, u32[]{:S(2)}) copy-start(f32[1024]{0:T(1024)} %param.17) | copy-start | bytes 12292
  25.6 37.2 %copy-start.4 = (s32[8,64]{1,0:T(8,128)S(1)}, s32[8,64]{1,0:T(8,128)}, u32[]{:S(2)}) copy-start(s32[8,64]{1,0:T(8,128)} %codes.1) | copy-start | bytes 6148
  38.2 24.6 %copy-start = (bf16[1024,1024]{1,0:T(8,128)(2,1)S(1)}, bf16[1024,1024]{1,0:T(8,128)(2,1)}, u32[]{:S(2)}) copy-start(bf16[1024,1024]{1,0:T(8,128)(2,1)} %out_buf.1) | copy-start | bytes 6291460
  38.2 24.6 %copy-start.6 = (f32[16]{0:T(128)S(1)}, f32[16]{0:T(128)}, u32[]{:S(2)}) copy-start(f32[16]{0:T(128)} %scale_ref.3) | copy-start | bytes 196

commit v5 on v4

--- a/solution.py
+++ b/solution.py
@@ -146,10 +146,7 @@
     turned = codes[...].astype(f32).T
     for f in range(8):
         hot = jnp.where(turned[:, f : f + 1].astype(jnp.int32) == iota((64, D), 1), f32(1.0), f32(0.0)).astype(bf16)
-        attn[64 * f : 64 * (f + 1), :] = hot
-    chosen[...] = jnp.dot(attn[...], codebook[...], preferred_element_type=f32).astype(bf16)
-    chosen_copy = pltpu.make_async_copy(chosen, chosen_hbm, chosen_sem)
-    chosen_copy.start()
+        o[64 * f : 64 * (f + 1), :] = hot
     half = D // 2
     one = f32(1.0)
     nil = f32(0.0)
@@ -175,6 +172,8 @@
     causal = (iota((256, 256), 0) & 127) >= (iota((256, 256), 1) & 127)
     for g in range(4):
         q, k, v = project(normed[...], qkv_buf, scale_ref, averager, g)
+        part = slice(g * GROUP, (g + 1) * GROUP)
+        chosen[:, part] = jnp.dot(o[...], codebook[:, part], preferred_element_type=f32).astype(bf16)
         for pair in range(2):
             lanes = slice(pair * PAIR, (pair + 1) * PAIR)
             for p in range(0, 4, 2):
@@ -194,6 +193,8 @@
                 for n, rows in enumerate((one_rows, two_rows)):
                     ratio = weighted_mean(w[n * 128 : (n + 1) * 128], value_pair(v[rows, lanes]))
                     attn[rows, g * GROUP + lanes.start : g * GROUP + lanes.stop] = ratio
+    chosen_copy = pltpu.make_async_copy(chosen, chosen_hbm, chosen_sem)
+    chosen_copy.start()
     want = iota((256, 256), 0)
     source = (want & 3) * 64 + (want >> 2)
     move = jnp.where(iota((256, 256), 1) == source, one, nil).astype(bf16)

time: 97.1 us -> 95.7 us (0.986)
  Pallas kernels: 26.1 us -> 24.7 us
    pallas_call x1, Pallas kernels: 11.1 us -> 9.66 us  [shards(): pl.pallas_call(temporal_kernel, out_shape=[jax.ShapeDtypeStruct((512, D),...]
where the time goes in v5:
time: 95.7 us; the launch traced here: 95.4 us
  blocking collectives  69.7 us (73%)
  Pallas kernels  24.7 us (26%)
    all_to_all x1, blocking collectives, shards(): x = lax.all_to_all(frames_in, 'patch', 0, 0, tiled=True).reshape(512, D)  24.9 us
    all_to_all x1, blocking collectives, shards(): lax.all_to_all(stream.reshape(128, 8, 512), ('tm', 'patch'), 0, 0, tiled=...  24.5 us
    all_to_all x1, blocking collectives, shards(): output = lax.all_to_all(output.reshape(16, 32, D), 'tm', 0, 0, tiled=True)  20.3 us
    pallas_call x1, Pallas kernels, shards(): pl.pallas_call(spatial_kernel, out_shape=jax.ShapeDtypeStruct((16, 8, 8,...  12.6 us
    pallas_call x1, Pallas kernels, shards(): pl.pallas_call(temporal_kernel, out_shape=[jax.ShapeDtypeStruct((512, D),...  9.66 us
    pallas_call x1, Pallas kernels, shards(): pl.pallas_call(final_kernel, out_shape=[jax.ShapeDtypeStruct((512, D), bf...  2.5 us

profile of v5, /device:TPU:1, one launch (start us, length us, event | category | flops | bytes accessed | tf_op | source)
XLA Modules:
  0.0 95.4 jit_solution(2023948753355200320)
XLA Ops:
  0.6 0.0 copy-start.5
  0.6 0.0 copy-start.2
  0.6 0.0 slice-start
  0.7 24.9 %all_to_all.15 = bf16[8,64,1024]{2,1,0:T(8,128)(2,1)S(1)} all-to-all(bf16[8,64,1024]{2,1,0:T(8,128)(2,1)} %param.11), channel_id=1, replica_groups=mesh['tm'=16,'patch'=8] {'patch'}, dimensions={0} | all-to-all | bytes 2097152 | tf_op jit(solution)/shard_map/all_to_all | solution.py:259
  25.6 0.0 copy-done.5
  25.6 0.0 copy-done.2
  25.6 0.0 slice-start.1
  25.6 0.0 copy-start.1
  25.6 0.0 copy-start.3
  25.6 0.0 copy-start.4
  25.6 12.6 %spatial.1 = bf16[16,8,8,512]{3,2,1,0:T(8,128)(2,1)S(1)} custom-call(bf16[512,1024]{1,0:T(8,128)(2,1)S(1)} %bitcast.9, f32[1,1024]{1,0:T(1,128)S(1)} %bitcast.12, f32[16]{0:T(128)S(1)} %copy-done.5, bf16[1024,3072]{1,0:T(8,128)(2,1)} %qkv_hbm.1, bf16[1024,1024]{1,0:T(8,128)(2,1)} %out_hbm.1), custom_call_target="tpu_custom_call" | custom-call | flops 10000000000 | bytes 10000000 | tf_op jit(solution)/shard_map/spatial/pallas_call | solution.py:261
  38.2 0.0 copy-start
  38.2 0.0 copy-start.6
  38.2 24.5 %all_to_all.16.x = bf16[128,8,512]{2,1,0:T(8,128)(2,1)S(1)} all-to-all(bf16[128,8,512]{2,1,0:T(8,128)(2,1)S(1)} %bitcast.8), channel_id=1, replica_groups=mesh['tm'=16,'patch'=8] {'tm','patch'}, dimensions={0} | all-to-all | bytes 2097152 | tf_op jit(solution)/shard_map/all_to_all | solution.py:274
  62.7 0.0 slice-done
  62.7 0.0 slice-done.1
  62.7 0.0 copy-done.1
  62.7 0.0 copy-done.3
  62.8 0.0 copy-done.4
  62.8 0.0 copy-done
  62.8 0.0 copy-done.6
  62.8 9.7 %temporal.1 = (bf16[512,1024]{1,0:T(8,128)(2,1)S(1)}, bf16[512,1024]{1,0:T(8,128)(2,1)}) custom-call(bf16[128,8,512]{2,1,0:T(8,128)(2,1)S(1)} %all_to_all.16.x, f32[1,1024]{1,0:T(1,128)S(1)} %bitcast.13, f32[16]{0:T(128)S(1)} %copy-done.6, bf16[1024,3072]{1,0:T(8,128)(2,1)S(1)} %bitcast.11, bf16[1024,1024]{1,0:T(8,128)(2,1)S(1)} %copy-done, ...), custom_call_target="tpu_custom_call" | custom-call | flops 8000000000 | bytes 10000000 | tf_op jit(solution)/shard_map/temporal/pallas_call | solution.py:275
  72.5 20.3 %all_to_all.17.x_ref = bf16[16,32,1024]{2,1,0:T(8,128)(2,1)S(1)} all-to-all(bf16[16,32,1024]{2,1,0:T(8,128)(2,1)S(1)} %bitcast.7), channel_id=1, replica_groups=mesh['tm'=16,'patch'=8] {'tm'}, dimensions={0} | all-to-all | bytes 2097152 | tf_op jit(solution)/shard_map/all_to_all | solution.py:288
  92.8 2.5 %final.1 = (bf16[512,1024]{1,0:T(8,128)(2,1)}, bf16[512,1024]{1,0:T(8,128)(2,1)}) custom-call(bf16[16,32,1024]{2,1,0:T(8,128)(2,1)S(1)} %all_to_all.17.x_ref, bf16[512,1024]{1,0:T(8,128)(2,1)} %get-tuple-element.7.chosen_hbm), custom_call_target="tpu_custom_call", output_to_operand_aliasing={{1}: (1, {})} | custom-call | flops 600000000 | bytes 4000000 | tf_op jit(solution)/shard_map/final/pallas_call | solution.py:289
  (1 shorter events, 0.0 us)
Async XLA Ops:
  0.6 24.9 %copy-start.5 = (f32[16]{0:T(128)S(1)}, f32[16]{0:T(128)}, u32[]{:S(2)}) copy-start(f32[16]{0:T(128)} %scale_ref.2) | copy-start | bytes 196
  0.6 24.9 %copy-start.2 = (f32[1024]{0:T(1024)S(1)}, f32[1024]{0:T(1024)}, u32[]{:S(2)}) copy-start(f32[1024]{0:T(1024)} %param.13) | copy-start | bytes 12292
  0.6 62.1 %slice-start = ((s8[6291456]{0:T(1024)(128)(4,1)}), s8[4194304]{0:T(1024)(128)(4,1)S(1)}, s32[]{:S(2)}) async-start(s8[6291456]{0:T(1024)(128)(4,1)} %bitcast.10), calls=%async_computation.3 | async-start | bytes 8388608
  25.6 37.2 %slice-start.1 = ((s8[6291456]{0:T(1024)(128)(4,1)}), s8[2097152]{0:T(1024)(128)(4,1)S(1)}, s32[]{:S(2)}) async-start(s8[6291456]{0:T(1024)(128)(4,1)} %bitcast.10), calls=%async_computation.4 | async-start | bytes 4194304
  25.6 37.2 %copy-start.1 = (bf16[1024,1024]{1,0:T(8,128)(2,1)S(1)}, bf16[1024,1024]{1,0:T(8,128)(2,1)}, u32[]{:S(2)}) copy-start(bf16[1024,1024]{1,0:T(8,128)(2,1)} %codebook.1) | copy-start | bytes 6291460
  25.6 37.2 %copy-start.3 = (f32[1024]{0:T(1024)S(1)}, f32[1024]{0:T(1024)}, u32[]{:S(2)}) copy-start(f32[1024]{0:T(1024)} %param.17) | copy-start | bytes 12292
  25.6 37.2 %copy-start.4 = (s32[8,64]{1,0:T(8,128)S(1)}, s32[8,64]{1,0:T(8,128)}, u32[]{:S(2)}) copy-start(s32[8,64]{1,0:T(8,128)} %codes.1) | copy-start | bytes 6148
  38.2 24.6 %copy-start = (bf16[1024,1024]{1,0:T(8,128)(2,1)S(1)}, bf16[1024,1024]{1,0:T(8,128)(2,1)}, u32[]{:S(2)}) copy-start(bf16[1024,1024]{1,0:T(8,128)(2,1)} %out_buf.1) | copy-start | bytes 6291460
  38.2 24.6 %copy-start.6 = (f32[16]{0:T(128)S(1)}, f32[16]{0:T(128)}, u32[]{:S(2)}) copy-start(f32[16]{0:T(128)} %scale_ref.3) | copy-start | bytes 196

commit v6 on v5

--- a/solution.py
+++ b/solution.py
@@ -140,8 +140,8 @@
 
 
 def temporal_kernel(
-    x, gain, scale_ref, qkv_buf, out_buf, codes, codebook, o_hbm, chosen_hbm,
-    stream, normed, attn, o, chosen, o_sems, chosen_sem,
+    x, gain, scale_ref, qkv_buf, out_buf, codes, codebook, o, chosen_hbm,
+    stream, normed, attn, chosen, chosen_sem,
 ):
     turned = codes[...].astype(f32).T
     for f in range(8):
@@ -198,7 +198,6 @@
     want = iota((256, 256), 0)
     source = (want & 3) * 64 + (want >> 2)
     move = jnp.where(iota((256, 256), 1) == source, one, nil).astype(bf16)
-    stores = []
     for b in range(2):
         pick = [slice(p * 128 + 64 * b, p * 128 + 64 * (b + 1)) for p in range(4)]
         mixed = jnp.concatenate([attn[rows, :] for rows in pick], 0)
@@ -206,11 +205,6 @@
         output = (base + jnp.dot(mixed, out_buf[...], preferred_element_type=f32)).astype(bf16)
         rows = pl.ds(256 * b, 256)
         o[rows, :] = jnp.dot(move, output, preferred_element_type=f32).astype(bf16)
-        store = pltpu.make_async_copy(o.at[rows, :], o_hbm.at[rows, :], o_sems.at[b])
-        store.start()
-        stores.append(store)
-    for store in stores:
-        store.wait()
     chosen_copy.wait()
 
 
@@ -276,11 +270,8 @@
         temporal_kernel,
         out_shape=[jax.ShapeDtypeStruct((512, D), bf16)] * 2,
         in_specs=[VM, VM, SM, VM, VM, VM, VM],
-        out_specs=[HBM, HBM],
-        scratch_shapes=[
-            pltpu.VMEM((512, D), f32), tall, tall, tall, tall,
-            pltpu.SemaphoreType.DMA((2,)), pltpu.SemaphoreType.DMA,
-        ],
+        out_specs=[VM, HBM],
+        scratch_shapes=[pltpu.VMEM((512, D), f32), tall, tall, tall, pltpu.SemaphoreType.DMA],
         compiler_params=params(20_000_000),
         cost_estimate=cost(4, 10),
         name="temporal",

time: 95.7 us -> 95.5 us (level)
  no operation moved by 1% of the time
where the time goes in v6:
time: 95.5 us; the launch traced here: 95.3 us
  blocking collectives  69.7 us (73%)
  Pallas kernels  24.6 us (26%)
    all_to_all x1, blocking collectives, shards(): x = lax.all_to_all(frames_in, 'patch', 0, 0, tiled=True).reshape(512, D)  24.9 us
    all_to_all x1, blocking collectives, shards(): lax.all_to_all(stream.reshape(128, 8, 512), ('tm', 'patch'), 0, 0, tiled=...  24.5 us
    all_to_all x1, blocking collectives, shards(): output = lax.all_to_all(output.reshape(16, 32, D), 'tm', 0, 0, tiled=True)  20.3 us
    pallas_call x1, Pallas kernels, shards(): pl.pallas_call(spatial_kernel, out_shape=jax.ShapeDtypeStruct((16, 8, 8,...  12.6 us
    pallas_call x1, Pallas kernels, shards(): pl.pallas_call(temporal_kernel, out_shape=[jax.ShapeDtypeStruct((512, D),...  9.49 us
    pallas_call x1, Pallas kernels, shards(): pl.pallas_call(final_kernel, out_shape=[jax.ShapeDtypeStruct((512, D), bf...  2.52 us

profile of v6, /device:TPU:1, one launch (start us, length us, event | category | flops | bytes accessed | tf_op | source)
XLA Modules:
  0.0 95.3 jit_solution(3359649505280073103)
XLA Ops:
  0.6 0.0 copy-start.5
  0.6 0.0 copy-start.2
  0.6 0.0 slice-start
  0.7 24.9 %all_to_all.15 = bf16[8,64,1024]{2,1,0:T(8,128)(2,1)S(1)} all-to-all(bf16[8,64,1024]{2,1,0:T(8,128)(2,1)} %param.11), channel_id=1, replica_groups=mesh['tm'=16,'patch'=8] {'patch'}, dimensions={0} | all-to-all | bytes 2097152 | tf_op jit(solution)/shard_map/all_to_all | solution.py:253
  25.6 0.0 copy-done.5
  25.6 0.0 copy-done.2
  25.6 0.0 slice-start.1
  25.6 0.0 copy-start.1
  25.6 0.0 copy-start.3
  25.6 0.0 copy-start.4
  25.6 12.6 %spatial.1 = bf16[16,8,8,512]{3,2,1,0:T(8,128)(2,1)S(1)} custom-call(bf16[512,1024]{1,0:T(8,128)(2,1)S(1)} %bitcast.9, f32[1,1024]{1,0:T(1,128)S(1)} %bitcast.12, f32[16]{0:T(128)S(1)} %copy-done.5, bf16[1024,3072]{1,0:T(8,128)(2,1)} %qkv_hbm.1, bf16[1024,1024]{1,0:T(8,128)(2,1)} %out_hbm.1), custom_call_target="tpu_custom_call" | custom-call | flops 10000000000 | bytes 10000000 | tf_op jit(solution)/shard_map/spatial/pallas_call | solution.py:255
  38.2 0.0 copy-start
  38.2 0.0 copy-start.6
  38.2 24.5 %all_to_all.16.x = bf16[128,8,512]{2,1,0:T(8,128)(2,1)S(1)} all-to-all(bf16[128,8,512]{2,1,0:T(8,128)(2,1)S(1)} %bitcast.8), channel_id=1, replica_groups=mesh['tm'=16,'patch'=8] {'tm','patch'}, dimensions={0} | all-to-all | bytes 2097152 | tf_op jit(solution)/shard_map/all_to_all | solution.py:268
  62.7 0.0 slice-done
  62.7 0.0 slice-done.1
  62.7 0.0 copy-done.1
  62.7 0.0 copy-done.3
  62.8 0.0 copy-done.4
  62.8 0.0 copy-done
  62.8 0.0 copy-done.6
  62.8 9.5 %temporal.1 = (bf16[512,1024]{1,0:T(8,128)(2,1)S(1)}, bf16[512,1024]{1,0:T(8,128)(2,1)}) custom-call(bf16[128,8,512]{2,1,0:T(8,128)(2,1)S(1)} %all_to_all.16.x, f32[1,1024]{1,0:T(1,128)S(1)} %bitcast.13, f32[16]{0:T(128)S(1)} %copy-done.6, bf16[1024,3072]{1,0:T(8,128)(2,1)S(1)} %bitcast.11, bf16[1024,1024]{1,0:T(8,128)(2,1)S(1)} %copy-done, ...), custom_call_target="tpu_custom_call" | custom-call | flops 8000000000 | bytes 10000000 | tf_op jit(solution)/shard_map/temporal/pallas_call | solution.py:269
  72.3 20.3 %all_to_all.17.x_ref = bf16[16,32,1024]{2,1,0:T(8,128)(2,1)S(1)} all-to-all(bf16[16,32,1024]{2,1,0:T(8,128)(2,1)S(1)} %bitcast.7), channel_id=1, replica_groups=mesh['tm'=16,'patch'=8] {'tm'}, dimensions={0} | all-to-all | bytes 2097152 | tf_op jit(solution)/shard_map/all_to_all | solution.py:279
  92.6 2.5 %final.1 = (bf16[512,1024]{1,0:T(8,128)(2,1)}, bf16[512,1024]{1,0:T(8,128)(2,1)}) custom-call(bf16[16,32,1024]{2,1,0:T(8,128)(2,1)S(1)} %all_to_all.17.x_ref, bf16[512,1024]{1,0:T(8,128)(2,1)} %get-tuple-element.7.chosen_hbm), custom_call_target="tpu_custom_call", output_to_operand_aliasing={{1}: (1, {})} | custom-call | flops 600000000 | bytes 4000000 | tf_op jit(solution)/shard_map/final/pallas_call | solution.py:280
  (1 shorter events, 0.0 us)
Async XLA Ops:
  0.6 24.9 %copy-start.5 = (f32[16]{0:T(128)S(1)}, f32[16]{0:T(128)}, u32[]{:S(2)}) copy-start(f32[16]{0:T(128)} %scale_ref.2) | copy-start | bytes 196
  0.6 24.9 %copy-start.2 = (f32[1024]{0:T(1024)S(1)}, f32[1024]{0:T(1024)}, u32[]{:S(2)}) copy-start(f32[1024]{0:T(1024)} %param.13) | copy-start | bytes 12292
  0.6 62.1 %slice-start = ((s8[6291456]{0:T(1024)(128)(4,1)}), s8[4194304]{0:T(1024)(128)(4,1)S(1)}, s32[]{:S(2)}) async-start(s8[6291456]{0:T(1024)(128)(4,1)} %bitcast.10), calls=%async_computation.3 | async-start | bytes 8388608
  25.6 37.2 %slice-start.1 = ((s8[6291456]{0:T(1024)(128)(4,1)}), s8[2097152]{0:T(1024)(128)(4,1)S(1)}, s32[]{:S(2)}) async-start(s8[6291456]{0:T(1024)(128)(4,1)} %bitcast.10), calls=%async_computation.4 | async-start | bytes 4194304
  25.6 37.2 %copy-start.1 = (bf16[1024,1024]{1,0:T(8,128)(2,1)S(1)}, bf16[1024,1024]{1,0:T(8,128)(2,1)}, u32[]{:S(2)}) copy-start(bf16[1024,1024]{1,0:T(8,128)(2,1)} %codebook.1) | copy-start | bytes 6291460
  25.6 37.2 %copy-start.3 = (f32[1024]{0:T(1024)S(1)}, f32[1024]{0:T(1024)}, u32[]{:S(2)}) copy-start(f32[1024]{0:T(1024)} %param.17) | copy-start | bytes 12292
  25.6 37.2 %copy-start.4 = (s32[8,64]{1,0:T(8,128)S(1)}, s32[8,64]{1,0:T(8,128)}, u32[]{:S(2)}) copy-start(s32[8,64]{1,0:T(8,128)} %codes.1) | copy-start | bytes 6148
  38.2 24.6 %copy-start = (bf16[1024,1024]{1,0:T(8,128)(2,1)S(1)}, bf16[1024,1024]{1,0:T(8,128)(2,1)}, u32[]{:S(2)}) copy-start(bf16[1024,1024]{1,0:T(8,128)(2,1)} %out_buf.1) | copy-start | bytes 6291460
  38.2 24.6 %copy-start.6 = (f32[16]{0:T(128)S(1)}, f32[16]{0:T(128)}, u32[]{:S(2)}) copy-start(f32[16]{0:T(128)} %scale_ref.3) | copy-start | bytes 196
